TPU v7x, 512 devices: a whole 4x8x8 slice. The times are simulated.
512 devices in a mesh: blk: 128 (over z, y, core), sub: 4 (over x).
Axes of the slice: x: 4, y: 8, z: 8, core: 2. Of those that a mesh axis runs over, the one named last changes fastest.
Arguments:
- populations: float32 [27, 512, 32, 128], P(None, 'blk', 'sub')
- destination: int32 [128, 4, 512, 1], P('blk', 'sub'), may hold values from 0 to 127; in each aligned block of 512 rows (0 to 511, 512 to 1023, ..., all dimensions but the last counted through in order) at most 8 rows name the same one
- base_cell: int32 [128, 4, 512], P('blk', 'sub'), may hold values from 0 to 2687
- offsets: float32 [128, 4, 3, 512], P('blk', 'sub'), may hold values from 0 to 1
- target: float32 [128, 4, 3, 512], P('blk', 'sub'), may hold values from -0.6 to 0.6
Outputs:
- read: float32 [27, 512, 32, 128], P(None, 'blk', 'sub')
- marker_force: float32 [128, 4, 3, 512], P('blk', 'sub')
Inputs may be any that keep to these rules, and one draw needn't show every extreme that they name: `destination`: in every draw the markers of one device name each index of blk at most 8 times, and some device names some index exactly 8 times. `base_cell`: decodes as (x0 (8 - 1) + z0) * 128 + y0 with x0 < 3 and z0 < 7.
All inputs are finite; a program needn't handle non-finite values.
Results may differ from a plain program's by a relative error of at most 0.0003.
Values sent between devices are 32-bit elements; how exact they have to be, the bound alone decides.
No kernel may reach another device: no remote copies, remote signals or barrier semaphores. Data moves between devices by JAX's collectives and lax.ppermute only.
A program may use at most 64 MiB of HBM per device.

v0:
```python
import jax
import jax.numpy as jnp
import numpy as np
from jax import lax
from jax.sharding import PartitionSpec as P

ZC = 8
CAP = 8


def extended(cells, sides, width):
    for axis, dim in sides:
        count = lax.axis_size(axis)
        head = lax.slice_in_dim(cells, 0, width, axis=dim)
        tail = lax.slice_in_dim(cells, cells.shape[dim] - width, cells.shape[dim], axis=dim)
        cells = jnp.concatenate(
            [
                lax.ppermute(tail, axis, [(i, (i + 1) % count) for i in range(count)]),
                cells,
                lax.ppermute(head, axis, [((i + 1) % count, i) for i in range(count)]),
            ],
            axis=dim,
        )
    return cells


def lattice():
    vel = np.array(
        [[a, b, c] for a in (-1, 0, 1) for b in (-1, 0, 1) for c in (-1, 0, 1)], dtype=np.int64
    )
    table = np.array([8.0 / 27.0, 2.0 / 27.0, 1.0 / 54.0, 1.0 / 216.0])
    return (vel, table[np.abs(vel).sum(1)])


def spread_axes(vec):
    return vec[:, None, None, None]


def collide(field, force, vel, wts):
    cx = spread_axes(jnp.asarray(vel[:, 0], jnp.float32))
    cy = spread_axes(jnp.asarray(vel[:, 1], jnp.float32))
    cz = spread_axes(jnp.asarray(vel[:, 2], jnp.float32))
    weight = spread_axes(jnp.asarray(wts, jnp.float32))
    rho = jnp.sum(field, axis=0)
    ux = (jnp.sum(field * cx, axis=0) + 0.5 * force[0]) / rho
    uy = (jnp.sum(field * cy, axis=0) + 0.5 * force[1]) / rho
    uz = (jnp.sum(field * cz, axis=0) + 0.5 * force[2]) / rho
    usq = ux * ux + uy * uy + uz * uz
    cu = cx * ux + cy * uy + cz * uz
    feq = weight * rho * (1.0 + 3.0 * cu + 4.5 * cu * cu - 1.5 * usq)
    cf = cx * force[0] + cy * force[1] + cz * force[2]
    uf = ux * force[0] + uy * force[1] + uz * force[2]
    source = weight * (3.0 * (cf - uf) + 9.0 * cu * cf)
    return field - 1.6 * (field - feq) + 0.2 * source


def fluid_velocity(field, vel):
    rho = jnp.sum(field, axis=0)
    parts = []
    for axis_pos in range(3):
        comp = spread_axes(jnp.asarray(vel[:, axis_pos], jnp.float32))
        parts.append(jnp.sum(field * comp, axis=0) / rho)
    return jnp.stack(parts)


def stencil(fracs, x_low, z_low, y_low, depth, width):
    result = []
    for dx in (0, 1):
        for dy in (0, 1):
            for dz in (0, 1):
                wx = fracs[0] if dx else 1.0 - fracs[0]
                wy = fracs[1] if dy else 1.0 - fracs[1]
                wz = fracs[2] if dz else 1.0 - fracs[2]
                flat = ((x_low + dx) * depth + z_low + dz) * width + (y_low + dy) % width
                result.append((wx * wy * wz, flat.astype(jnp.int32)))
    return result


def decode(cells, width):
    y_low = cells % width
    rest = cells // width
    return (rest // (ZC - 1), rest % (ZC - 1), y_low)


def body(populations, destination, base_cell, offsets, target):
    vel, wts = lattice()
    xdev, zdev, ny = (populations.shape[1], populations.shape[2], populations.shape[3])
    nblk = lax.axis_size("blk")
    velocity = fluid_velocity(populations, vel).reshape(3, -1)
    owner = destination[0, 0, :, 0]
    cells = base_cell[0, 0]
    markers = cells.shape[0]
    onehot = (owner[:, None] == jnp.arange(nblk, dtype=jnp.int32)[None, :]).astype(jnp.int32)
    rank = jnp.sum((jnp.cumsum(onehot, axis=0) - onehot) * onehot, axis=1)
    slot = owner * CAP + rank
    payload = jnp.concatenate(
        [offsets[0, 0], target[0, 0], jnp.ones((1, markers), jnp.float32)], axis=0
    )
    send_floats = jnp.zeros((7, nblk * CAP), jnp.float32).at[:, slot].set(payload)
    send_floats = jnp.transpose(send_floats.reshape(7, nblk, CAP), (1, 0, 2))
    send_cells = jnp.zeros((nblk * CAP,), jnp.int32).at[slot].set(cells).reshape(nblk, 1, CAP)
    floats = lax.all_to_all(send_floats, "blk", split_axis=0, concat_axis=0, tiled=True)
    ints = lax.all_to_all(send_cells, "blk", split_axis=0, concat_axis=0, tiled=True)
    x_low, z_low, y_low = decode(ints[:, 0], ny)
    fracs = (floats[:, 0], floats[:, 1], floats[:, 2])
    interp = jnp.zeros((3,) + x_low.shape, jnp.float32)
    for interpolate_weight, interpolate_flat in stencil(fracs, x_low, z_low, y_low, zdev, ny):
        interp = interp + interpolate_weight[None] * velocity[:, interpolate_flat]
    pull = 2.0 * (floats[:, 3:6] - jnp.moveaxis(interp, 0, 1)) * floats[:, 6:7]
    force_here = pull
    x_low, z_low, y_low = decode(ints[:, 0], ny)
    fracs = (floats[:, 0], floats[:, 1], floats[:, 2])
    pull = jnp.moveaxis(force_here, 1, 0)
    field = jnp.zeros((3, xdev * zdev * ny), jnp.float32)
    for weight, flat in stencil(fracs, x_low, z_low, y_low, zdev, ny):
        field = field.at[:, flat.reshape(-1)].add((weight[None] * pull).reshape(3, -1))
    force = field.reshape(3, xdev, zdev, ny)
    post = collide(populations, force, vel, wts)
    pieces = []
    padded = extended(post, (("blk", 1), ("sub", 2)), 1)
    for i in range(27):
        step_x, step_y, step_z = (int(vel[i, 0]), int(vel[i, 1]), int(vel[i, 2]))
        piece = padded[i, 1 - step_x : 1 - step_x + xdev, 1 - step_z : 1 - step_z + zdev, :]
        pieces.append(jnp.roll(piece, step_y, axis=2))
    read = jnp.stack(pieces)
    back = lax.all_to_all(force_here, "blk", split_axis=0, concat_axis=0, tiled=True)
    marker_force = jnp.transpose(back, (1, 0, 2)).reshape(3, -1)[:, slot]
    return (read, marker_force[None, None])


def solution(mesh):
    in_specs = (
        P(None, "blk", "sub", None),
        P("blk", "sub", None, None),
        P("blk", "sub", None),
        P("blk", "sub", None, None),
        P("blk", "sub", None, None),
    )
    out_specs = (P(None, "blk", "sub", None), P("blk", "sub", None, None))
    return jax.shard_map(body, mesh=mesh, in_specs=in_specs, out_specs=out_specs, check_vma=False)
```

profile of v0, /device:TPU:1, one launch (start us, length us, event | category | flops | bytes accessed | tf_op | source)
XLA Modules:
  0.0 215.9 jit_solution(9237377067269387726)
XLA Ops:
  3.4 2.6 %scatter_custom_fusion = s32[1024]{0:T(1024)S(1)} fusion(s32[512]{0:T(512)S(1)} %bitcast.372, s32[512]{0:T(512)} %bitcast.376, s32[]{:T(128)} %constant.139.clone.1), kind=kCustom, calls=%fused_computation.228 | custom fusion | bytes 4608 | tf_op jit(solution)/shard_map/scatter | solution.py:101
  6.7 18.4 %all-to-all-start = ((s32[128,1,8]{2,1,0:T(1,128)}), s32[128,1,8]{2,1,0:T(1,128)S(1)}, u32[]{:S(2)}, u32[]{:S(2)}) async-start(s32[128,1,8]{2,1,0:T(1,128)} %bitcast.9), calls=%async_computation | async-start | bytes 131072 | tf_op jit(solution)/shard_map/all_to_all | solution.py:103
  28.3 1.8 scatter_custom_fusion.1
  30.2 1.6 copy.170
  31.8 4.8 %all-to-all-done = s32[128,1,8]{2,1,0:T(1,128)S(1)} async-done(((s32[128,1,8]{2,1,0:T(1,128)}), s32[128,1,8]{2,1,0:T(1,128)S(1)}, u32[]{:S(2)}, u32[]{:S(2)}) %all-to-all-start) | async-done | bytes 4128 | tf_op jit(solution)/shard_map/all_to_all | solution.py:103
  36.5 9.0 %all-to-all-start.1 = ((f32[128,7,8]{2,1,0:T(8,128)}), f32[128,7,8]{2,1,0:T(8,128)S(1)}, u32[]{:S(2)}, u32[]{:S(2)}) async-start(f32[128,7,8]{2,1,0:T(8,128)} %bitcast.13), calls=%async_computation.1 | async-start | bytes 1048576 | tf_op jit(solution)/shard_map/all_to_all | solution.py:102
  51.5 4.0 %gather_fusion.5 = f32[1024,3]{1,0:T(8,128)} fusion(f32[3,4096]{0,1:T(8,128)S(1)} %copy.175, s32[1024]{0:T(1024)S(1)} %get-tuple-element.111), kind=kCustom, calls=%fused_computation.5 | custom fusion | bytes 28672 | tf_op jit(solution)/shard_map/gather | solution.py:108
  56.7 4.0 %gather_fusion.6 = f32[1024,3]{1,0:T(8,128)} fusion(f32[3,4096]{0,1:T(8,128)S(1)} %copy.175, s32[1024]{0:T(1024)S(1)} %get-tuple-element.110), kind=kCustom, calls=%fused_computation.6 | custom fusion | bytes 28672 | tf_op jit(solution)/shard_map/gather | solution.py:108
  61.9 4.0 %gather_fusion.1 = f32[1024,3]{1,0:T(8,128)} fusion(f32[3,4096]{0,1:T(8,128)S(1)} %copy.175, s32[1024]{0:T(1024)S(1)} %get-tuple-element.115), kind=kCustom, calls=%fused_computation.1 | custom fusion | bytes 28672 | tf_op jit(solution)/shard_map/gather | solution.py:108
  67.2 4.0 %gather_fusion.2 = f32[1024,3]{1,0:T(8,128)} fusion(f32[3,4096]{0,1:T(8,128)S(1)} %copy.175, s32[1024]{0:T(1024)S(1)} %get-tuple-element.114), kind=kCustom, calls=%fused_computation.2 | custom fusion | bytes 28672 | tf_op jit(solution)/shard_map/gather | solution.py:108
  72.4 4.0 %gather_fusion.3 = f32[1024,3]{1,0:T(8,128)} fusion(f32[3,4096]{0,1:T(8,128)S(1)} %copy.175, s32[1024]{0:T(1024)S(1)} %get-tuple-element.113), kind=kCustom, calls=%fused_computation.3 | custom fusion | bytes 28672 | tf_op jit(solution)/shard_map/gather | solution.py:108
  76.4 1.2 copy.186
  77.7 4.0 %gather_fusion.4 = f32[1024,3]{1,0:T(8,128)} fusion(f32[3,4096]{0,1:T(8,128)S(1)} %copy.175, s32[1024]{0:T(1024)S(1)} %get-tuple-element.112), kind=kCustom, calls=%fused_computation.4 | custom fusion | bytes 28672 | tf_op jit(solution)/shard_map/gather | solution.py:108
  81.7 1.2 copy.189
  82.9 4.0 %gather_fusion.7 = f32[1024,3]{1,0:T(8,128)} fusion(f32[3,4096]{0,1:T(8,128)S(1)} %copy.175, s32[1024]{0:T(1024)S(1)} %get-tuple-element.109), kind=kCustom, calls=%fused_computation.7 | custom fusion | bytes 28672 | tf_op jit(solution)/shard_map/gather | solution.py:108
  86.9 1.2 copy.198
  88.1 4.0 %gather_fusion = f32[1024,3]{1,0:T(8,128)} fusion(f32[3,4096]{0,1:T(8,128)S(1)} %copy.175, s32[1024]{0:T(1024)S(1)} %broadcast_clamp_fusion.7), kind=kCustom, calls=%fused_computation | custom fusion | bytes 28672 | tf_op jit(solution)/shard_map/gather | solution.py:108
  103.8 6.9 %scatter_custom_fusion.2 = f32[3,4096]{0,1:T(8,128)S(1)} fusion(s32[1024]{0:T(1024)S(1)} %bitcast.375, f32[1024,3]{1,0:T(8,128)} %copy.201, f32[]{:T(128)} %constant.138.clone.1), kind=kCustom, calls=%fused_computation.22 | custom fusion | flops 3072 | bytes 49664 | tf_op jit(solution)/shard_map/scatter-add | solution.py:116
  110.7 6.8 %scatter_fusion = f32[3,4096]{0,1:T(8,128)S(1)} fusion(f32[3,4096]{0,1:T(8,128)S(1)} %scatter_custom_fusion.2, s32[1024]{0:T(1024)S(1)} %bitcast.370, f32[1024,3]{1,0:T(8,128)S(1)} %copy.203), kind=kCustom, calls=%fused_computation.12 | custom fusion | flops 3072 | bytes 40960 | tf_op jit(solution)/shard_map/scatter-add | solution.py:116
  117.5 7.2 %scatter_fusion.1 = f32[3,4096]{0,1:T(8,128)S(1)} fusion(f32[3,4096]{0,1:T(8,128)S(1)} %scatter_fusion, s32[1024]{0:T(1024)S(1)} %bitcast.369, f32[1024,3]{1,0:T(8,128)} %copy.205), kind=kCustom, calls=%fused_computation.13 | custom fusion | flops 3072 | bytes 40960 | tf_op jit(solution)/shard_map/scatter-add | solution.py:116
  124.7 7.4 %scatter_fusion.2 = f32[3,4096]{0,1:T(8,128)S(1)} fusion(f32[3,4096]{0,1:T(8,128)S(1)} %scatter_fusion.1, s32[1024]{0:T(1024)S(1)} %bitcast.366, f32[1024,3]{1,0:T(8,128)} %copy.207), kind=kCustom, calls=%fused_computation.14 | custom fusion | flops 3072 | bytes 40960 | tf_op jit(solution)/shard_map/scatter-add | solution.py:116
  132.2 7.2 %scatter_fusion.3 = f32[3,4096]{0,1:T(8,128)S(1)} fusion(f32[3,4096]{0,1:T(8,128)S(1)} %scatter_fusion.2, s32[1024]{0:T(1024)S(1)} %bitcast.368, f32[1024,3]{1,0:T(8,128)} %copy.209), kind=kCustom, calls=%fused_computation.15 | custom fusion | flops 3072 | bytes 40960 | tf_op jit(solution)/shard_map/scatter-add | solution.py:116
  139.4 7.2 %scatter_fusion.4 = f32[3,4096]{0,1:T(8,128)S(1)} fusion(f32[3,4096]{0,1:T(8,128)S(1)} %scatter_fusion.3, s32[1024]{0:T(1024)S(1)} %bitcast.365, f32[1024,3]{1,0:T(8,128)} %copy.211), kind=kCustom, calls=%fused_computation.16 | custom fusion | flops 3072 | bytes 40960 | tf_op jit(solution)/shard_map/scatter-add | solution.py:116
  146.6 7.2 %scatter_fusion.5 = f32[3,4096]{0,1:T(8,128)S(1)} fusion(f32[3,4096]{0,1:T(8,128)S(1)} %scatter_fusion.4, s32[1024]{0:T(1024)S(1)} %bitcast.364, f32[1024,3]{1,0:T(8,128)} %copy.213), kind=kCustom, calls=%fused_computation.17 | custom fusion | flops 3072 | bytes 40960 | tf_op jit(solution)/shard_map/scatter-add | solution.py:116
  153.8 7.5 %scatter_fusion.6 = f32[3,4096]{0,1:T(8,128)S(1)} fusion(f32[3,4096]{0,1:T(8,128)S(1)} %scatter_fusion.5, s32[1024]{0:T(1024)S(1)} %bitcast.363, f32[1024,3]{1,0:T(8,128)} %copy.215), kind=kCustom, calls=%fused_computation.18 | custom fusion | flops 3072 | bytes 40960 | tf_op jit(solution)/shard_map/scatter-add | solution.py:116
  161.3 2.8 %slice_reduce_fusion.2 = (f32[4096]{0:T(1024)S(1)}, f32[4096]{0:T(1024)S(1)}, f32[4096]{0:T(1024)S(1)}) fusion(f32[3,4096]{0,1:T(8,128)S(1)} %scatter_fusion.6), kind=kLoop, calls=%fused_computation.21 | loop fusion | bytes 98304 | tf_op jit(solution)/shard_map/slice | solution.py:45
  164.9 3.5 %collective-permute-start = (f32[27,1,8,128]{3,2,1,0:T(8,128)S(1)}, f32[27,1,8,128]{3,2,1,0:T(8,128)S(1)}, u32[]{:S(2)}, u32[]{:S(2)}) collective-permute-start(f32[27,1,8,128]{3,2,1,0:T(8,128)S(1)} %get-tuple-element.71), channel_id=1, source_target_pairs={{0,4},{4,8},{8,12},{12,16},{16,20},{20,24},{24,28},{28,32},{32,36}... | collective-permute-start | bytes 331784 | tf_op jit(solution)/shard_map/ppermute | solution.py:18
  168.4 1.9 collective-permute-start.1
  170.3 4.4 %collective-permute-done.1 = f32[27,1,8,128]{3,2,1,0:T(8,128)S(1)} collective-permute-done((f32[27,1,8,128]{3,2,1,0:T(8,128)S(1)}, f32[27,1,8,128]{3,2,1,0:T(8,128)S(1)}, u32[]{:S(2)}, u32[]{:S(2)}) %collective-permute-start.1) | collective-permute-done | bytes 110624 | tf_op jit(solution)/shard_map/ppermute | solution.py:20
  174.8 4.5 %collective-permute-start.2 = (f32[27,6,1,128]{3,2,1,0:T(1,128)S(1)}, f32[27,6,1,128]{3,2,1,0:T(1,128)S(1)}, u32[]{:S(2)}, u32[]{:S(2)}) collective-permute-start(f32[27,6,1,128]{3,2,1,0:T(1,128)S(1)} %get-tuple-element.60), channel_id=1, source_target_pairs={{1,0},{2,1},{3,2},{0,3},{5,4},{6,5},{7,6},{4,7},{9,8},{10,9},{11,1... | collective-permute-start | bytes 248840 | tf_op jit(solution)/shard_map/ppermute | solution.py:20
  179.3 1.9 collective-permute-start.3
  181.4 28.3 %all_to_all.15 = f32[128,3,8]{2,1,0:T(4,128)S(1)} all-to-all(f32[128,3,8]{2,1,0:T(4,128)S(1)} %copy.216), channel_id=1, replica_groups=mesh['blk'=128,'sub'=4] {'blk'}, dimensions={0} | all-to-all | bytes 24576 | tf_op jit(solution)/shard_map/all_to_all | solution.py:126
  (166 shorter events, 35.8 us)
Async XLA Ops:
  0.6 25.3 %copy-start = (f32[27,4,8,128]{3,2,1,0:T(8,128)S(1)}, f32[27,4,8,128]{3,2,1,0:T(8,128)}, u32[]{:S(2)}) copy-start(f32[27,4,8,128]{3,2,1,0:T(8,128)} %param.12) | copy-start | bytes 1327108
  3.4 28.4 %copy-start.7 = (s32[512,1]{0,1:T(1,128)}, s32[512,1]{0,1:T(1,128)S(1)}, u32[]{:S(2)}) copy-start(s32[512,1]{0,1:T(1,128)S(1)} %compare_select_fusion.20) | copy-start | bytes 6148
  6.7 29.8 %all-to-all-start = ((s32[128,1,8]{2,1,0:T(1,128)}), s32[128,1,8]{2,1,0:T(1,128)S(1)}, u32[]{:S(2)}, u32[]{:S(2)}) async-start(s32[128,1,8]{2,1,0:T(1,128)} %bitcast.9), calls=%async_computation | async-start | bytes 131072 | tf_op jit(solution)/shard_map/all_to_all | solution.py:103
  26.8 0.6 copy-start.1
  26.8 0.6 copy-start.3
  26.8 0.6 copy-start.5
  36.5 56.8 %all-to-all-start.1 = ((f32[128,7,8]{2,1,0:T(8,128)}), f32[128,7,8]{2,1,0:T(8,128)S(1)}, u32[]{:S(2)}, u32[]{:S(2)}) async-start(f32[128,7,8]{2,1,0:T(8,128)} %bitcast.13), calls=%async_computation.1 | async-start | bytes 1048576 | tf_op jit(solution)/shard_map/all_to_all | solution.py:102
  161.2 2.9 %copy-start.2 = (f32[4,8,128]{2,1,0:T(8,128)S(1)}, f32[4,8,128]{2,1,0:T(8,128)}, u32[]{:S(2)}) copy-start(f32[4,8,128]{2,1,0:T(8,128)} %copy-done.1) | copy-start | bytes 49156
  161.3 2.9 %copy-start.4 = (f32[4,8,128]{2,1,0:T(8,128)S(1)}, f32[4,8,128]{2,1,0:T(8,128)}, u32[]{:S(2)}) copy-start(f32[4,8,128]{2,1,0:T(8,128)} %copy-done.3) | copy-start | bytes 49156
  161.3 2.9 %copy-start.6 = (f32[4,8,128]{2,1,0:T(8,128)S(1)}, f32[4,8,128]{2,1,0:T(8,128)}, u32[]{:S(2)}) copy-start(f32[4,8,128]{2,1,0:T(8,128)} %copy-done.5) | copy-start | bytes 49156
  161.3 2.9 %copy-start.8 = (f32[27]{0:T(128)S(1)}, f32[27]{0:T(128)}, u32[]{:S(2)}) copy-start(f32[27]{0:T(128)} %constant.157.clone) | copy-start | bytes 328
  161.3 2.9 %copy-start.9 = (f32[27]{0:T(128)S(1)}, f32[27]{0:T(128)}, u32[]{:S(2)}) copy-start(f32[27]{0:T(128)} %constant.158.clone) | copy-start | bytes 328
  161.3 2.9 %copy-start.10 = (f32[27]{0:T(128)S(1)}, f32[27]{0:T(128)}, u32[]{:S(2)}) copy-start(f32[27]{0:T(128)} %constant.159.clone) | copy-start | bytes 328
  161.3 2.9 %copy-start.12 = (f32[27]{0:T(128)S(1)}, f32[27]{0:T(128)}, u32[]{:S(2)}) copy-start(f32[27]{0:T(128)} %constant.160.clone) | copy-start | bytes 328
  164.9 5.4 %collective-permute-start = (f32[27,1,8,128]{3,2,1,0:T(8,128)S(1)}, f32[27,1,8,128]{3,2,1,0:T(8,128)S(1)}, u32[]{:S(2)}, u32[]{:S(2)}) collective-permute-start(f32[27,1,8,128]{3,2,1,0:T(8,128)S(1)} %get-tuple-element.71), channel_id=1, source_target_pairs={{0,4},{4,8},{8,12},{12,16},{16,20},{20,24},{24,28},{28,32},{32,36}... | collective-permute-start | bytes 331784 | tf_op jit(solution)/shard_map/ppermute | solution.py:18
  168.4 6.4 %collective-permute-start.1 = (f32[27,1,8,128]{3,2,1,0:T(8,128)S(1)}, f32[27,1,8,128]{3,2,1,0:T(8,128)S(1)}, u32[]{:S(2)}, u32[]{:S(2)}) collective-permute-start(f32[27,1,8,128]{3,2,1,0:T(8,128)S(1)} %get-tuple-element.72), channel_id=1, source_target_pairs={{4,0},{8,4},{12,8},{16,12},{20,16},{24,20},{28,24},{32,28},{36,32}... | collective-permute-start | bytes 331784 | tf_op jit(solution)/shard_map/ppermute | solution.py:20
  174.8 37.4 %collective-permute-start.2 = (f32[27,6,1,128]{3,2,1,0:T(1,128)S(1)}, f32[27,6,1,128]{3,2,1,0:T(1,128)S(1)}, u32[]{:S(2)}, u32[]{:S(2)}) collective-permute-start(f32[27,6,1,128]{3,2,1,0:T(1,128)S(1)} %get-tuple-element.60), channel_id=1, source_target_pairs={{1,0},{2,1},{3,2},{0,3},{5,4},{6,5},{7,6},{4,7},{9,8},{10,9},{11,1... | collective-permute-start | bytes 248840 | tf_op jit(solution)/shard_map/ppermute | solution.py:20
  179.3 32.9 %collective-permute-start.3 = (f32[27,6,1,128]{3,2,1,0:T(1,128)S(1)}, f32[27,6,1,128]{3,2,1,0:T(1,128)S(1)}, u32[]{:S(2)}, u32[]{:S(2)}) collective-permute-start(f32[27,6,1,128]{3,2,1,0:T(1,128)S(1)} %get-tuple-element.59), channel_id=1, source_target_pairs={{0,1},{1,2},{2,3},{3,0},{4,5},{5,6},{6,7},{7,4},{8,9},{9,10},{10,1... | collective-permute-start | bytes 248840 | tf_op jit(solution)/shard_map/ppermute | solution.py:18
  215.1 0.8 copy-start.11
where the time goes:
time: 217 us; the launch traced here: 216 us
  local copies, waits for them, and re-layouts  72.5 us (33%)
  other arithmetic  65.4 us (30%)
  starting transfers between devices  39.2 us (18%)
  blocking collectives  28.3 us (13%)
  waiting for transfers between devices  9.2 us (4%)
    scatter-add x8, other arithmetic, body(): field.at[:, flat.reshape(-1)].add((weight[None] * pull).reshape(3, -1))  57.4 us
    gather x16, local copies, waits for them, and re-layouts, body(): interp = interp + interpolate_weight[None] * velocity[:, interpolate_flat]  41.9 us
    all_to_all x1, blocking collectives, body(): lax.all_to_all(force_here, 'blk', split_axis=0, concat_axis=0, tiled=True)  28.3 us
    all_to_all x1, starting transfers between devices, body(): lax.all_to_all(send_cells, 'blk', split_axis=0, concat_axis=0, tiled=True)  18.4 us
    all_to_all x1, starting transfers between devices, body(): lax.all_to_all(send_floats, 'blk', split_axis=0, concat_axis=0, tiled=True)  8.98 us
    reshape x16, local copies, waits for them, and re-layouts, body(): (weight[None] * pull).reshape(3, -1)  8.6 us
    ppermute x2, starting transfers between devices, extended(): lax.ppermute(head, axis, [((i + 1) % count, i) for i in range(count)])  6.38 us
    ppermute x2, starting transfers between devices, extended(): lax.ppermute(tail, axis, [(i, (i + 1) % count) for i in range(count)])  5.42 us
  transfers between devices with their start and end apart: 6, of which 2 were waited for; matrix products, arithmetic and copies ran while one was open for 26% of the time, Pallas kernels for 0%

commit v1 on v0

v1 whole, which is shorter than its diff:
```python
import jax
import jax.numpy as jnp
import numpy as np
from jax import lax
from jax.experimental import pallas as pl
from jax.experimental.pallas import tpu as pltpu
from jax.sharding import PartitionSpec as P

CAP = 8
NB = 128
NY = 128
XD = 4
ZD = 8
M = 512
F32 = jnp.float32
BF16 = jnp.bfloat16
VEL = [(a, b, c) for a in (-1, 0, 1) for b in (-1, 0, 1) for c in (-1, 0, 1)]
WTS = [(8.0 / 27.0, 2.0 / 27.0, 1.0 / 54.0, 1.0 / 216.0)[abs(a) + abs(b) + abs(c)] for a, b, c in VEL]
UP_X = [i for i in range(27) if VEL[i][0] == 1]
DOWN_X = [i for i in range(27) if VEL[i][0] == -1]
UP_Z = [i for i in range(27) if VEL[i][2] == 1]
DOWN_Z = [i for i in range(27) if VEL[i][2] == -1]
LIMIT = 12 * 1024 * 1024


def iota(shape, dim):
    return lax.broadcasted_iota(jnp.int32, shape, dim)


def split(x):
    hi = x.astype(BF16)
    return hi, (x - hi.astype(F32)).astype(BF16)


def dot_nt(a, b):
    return lax.dot_general(a, b, (((1,), (1,)), ((), ())), preferred_element_type=F32)


def dot_nn(a, b):
    return lax.dot_general(a, b, (((1,), (0,)), ((), ())), preferred_element_type=F32)


def pack_kernel(dest_ref, cell_ref, offs_ref, targ_ref, send_ref, rank_ref):
    owner = dest_ref[...]
    hot = jnp.where(iota((NB, M), 0) == owner, 1.0, 0.0)
    hot16 = hot.astype(BF16)
    before = jnp.where(iota((M, M), 0) < iota((M, M), 1), 1.0, 0.0).astype(BF16)
    count = dot_nn(hot16, before)
    rank = jnp.sum(count * hot, axis=0, keepdims=True).astype(jnp.int32)
    rank_ref[...] = rank
    chosen = jnp.where(iota((CAP, M), 0) == rank, 1.0, 0.0)
    feats = [offs_ref[k] for k in range(3)] + [targ_ref[k] for k in range(3)]
    feats += [cell_ref[...].astype(F32), jnp.ones((1, M), F32)]
    table = jnp.concatenate([chosen * f for f in feats], axis=0)
    hi, lo = split(table)
    packed = dot_nt(hot16, hi) + dot_nt(hot16, lo)
    send_ref[...] = jnp.concatenate([packed, jnp.zeros((NB, 64), F32)], axis=1)


def moments(load):
    rho = jx = jy = jz = None

    def acc(total, term, sign):
        if sign == 0:
            return total
        if total is None:
            return term if sign > 0 else -term
        return total + term if sign > 0 else total - term

    for i in range(27):
        f = load(i)
        rho = acc(rho, f, 1)
        jx = acc(jx, f, VEL[i][0])
        jy = acc(jy, f, VEL[i][1])
        jz = acc(jz, f, VEL[i][2])
    return rho, jx, jy, jz


def velocity_kernel(pop_ref, vel_ref):
    comps = [[], [], []]
    for x in range(XD):
        rho, jx, jy, jz = moments(lambda i: pop_ref[i, x])
        for c, j in enumerate((jx, jy, jz)):
            comps[c].append(j / rho)
    low = jnp.concatenate([v for comp in comps for v in comp], axis=0)
    high = pltpu.roll(low, NY - 1, 1)
    hi, lo = split(jnp.concatenate([low, high], axis=0))
    vel_ref[...] = jnp.concatenate([hi, lo], axis=0)


def signed(vec, c):
    total = None
    for v, s in zip(vec, c):
        if s:
            term = v if s > 0 else -v
            total = term if total is None else total + term
    return total


def force_kernel(recv_ref, vel_ref, pop_ref, post_ref, back_ref, up_ref, down_ref):
    table = jnp.transpose(recv_ref[...])
    feat = [table[8 * k : 8 * k + 8] for k in range(8)]
    ox, oy, oz = feat[0], feat[1], feat[2]
    valid = feat[7]
    cell = feat[6].astype(jnp.int32)
    y_low = cell & (NY - 1)
    rest = cell >> 7
    x_low = jnp.where(rest >= 7, 1, 0) + jnp.where(rest >= 14, 1, 0)
    z_low = rest - 7 * x_low
    wx = [
        jnp.where(x_low == x, 1.0 - ox, 0.0) + jnp.where(x_low == x - 1, ox, 0.0)
        for x in range(XD)
    ]
    rows = iota((NY, NB), 0)
    zrow = iota((ZD, NB), 0)
    hot = [jnp.where(rows == y_low[r : r + 1], 1.0, 0.0).astype(BF16) for r in range(CAP)]
    hot = jnp.concatenate(hot, axis=1)
    looked = dot_nn(vel_ref[...], hot)
    looked = looked[:192] + looked[192:]
    pulls = [[], [], []]
    near, far = [], []
    for r in range(CAP):
        one = slice(r, r + 1)
        zl, fz, fy = z_low[one], oz[one], oy[one]
        wz = jnp.where(zrow == zl, 1.0 - fz, 0.0) + jnp.where(zrow == zl + 1, fz, 0.0)
        wz0, wz1 = wz * (1.0 - fy), wz * fy
        w0 = [wz0 * wx[x][one] for x in range(XD)]
        w1 = [wz1 * wx[x][one] for x in range(XD)]
        lanes = slice(NB * r, NB * r + NB)
        col0, col1 = [], []
        for c in range(3):
            total = None
            for x in range(XD):
                at = 32 * c + 8 * x
                term = looked[at : at + 8, lanes] * w0[x] + looked[96 + at : 104 + at, lanes] * w1[x]
                total = term if total is None else total + term
            interp = jnp.sum(total, axis=0, keepdims=True)
            pull = 2.0 * (feat[3 + c][one] - interp) * valid[one]
            pulls[c].append(pull)
            col0 += [w0[x] * pull for x in range(XD)]
            col1 += [w1[x] * pull for x in range(XD)]
        near.append(jnp.concatenate(col0, axis=0))
        far.append(jnp.concatenate(col1, axis=0))
    reply = jnp.concatenate([p for comp in pulls for p in comp] + [jnp.zeros((NB - 24, NB), F32)], axis=0)
    back_ref[...] = jnp.transpose(reply)
    amount = jnp.concatenate([jnp.concatenate(near, axis=1), jnp.concatenate(far, axis=1)], axis=0)
    hi, lo = split(amount)
    field = dot_nt(hi, hot) + dot_nt(lo, hot)
    field = field[:96] + pltpu.roll(field[96:], 1, 1)
    for x in range(XD):
        rho, jx, jy, jz = moments(lambda i: pop_ref[i, x])
        force = [field[32 * c + 8 * x : 32 * c + 8 * x + 8] for c in range(3)]
        inv = 1.0 / rho
        u = [(j + 0.5 * f) * inv for j, f in zip((jx, jy, jz), force)]
        usq = u[0] * u[0] + u[1] * u[1] + u[2] * u[2]
        uf = u[0] * force[0] + u[1] * force[1] + u[2] * force[2]
        base = 1.6 * rho * (1.0 - 1.5 * usq) - 0.6 * uf
        ru = [rho * v for v in u]
        g = [4.8 * a + 0.6 * f for a, f in zip(ru, force)]
        h = [7.2 * a + 1.8 * f for a, f in zip(ru, force)]
        for i in range(13, 27):
            if i == 13:
                posts = ((13, WTS[13] * base),)
            else:
                c = VEL[i]
                even = base + signed(u, c) * signed(h, c)
                odd = signed(g, c)
                posts = ((i, WTS[i] * (even + odd)), (26 - i, WTS[i] * (even - odd)))
            for k, term in posts:
                out = term - 0.6 * pop_ref[k, x]
                if VEL[k][1]:
                    out = pltpu.roll(out, VEL[k][1] % NY, 1)
                post_ref[k, x] = out
                if x == XD - 1 and VEL[k][0] == 1:
                    up_ref[UP_X.index(k)] = out
                if x == 0 and VEL[k][0] == -1:
                    down_ref[DOWN_X.index(k)] = out


def shifted(post_ref, low_ref, high_ref, i, x):
    at = x - VEL[i][0]
    if at < 0:
        return low_ref[UP_X.index(i)]
    if at >= XD:
        return high_ref[DOWN_X.index(i)]
    return post_ref[i, at]


def edge_kernel(post_ref, low_ref, high_ref, up_ref, down_ref):
    up, down = [], []
    for i in UP_Z:
        for x in range(XD):
            up.append(shifted(post_ref, low_ref, high_ref, i, x)[ZD - 1 :])
    for i in DOWN_Z:
        for x in range(XD):
            down.append(shifted(post_ref, low_ref, high_ref, i, x)[:1])
    up_ref[...] = jnp.concatenate(up, axis=0)
    down_ref[...] = jnp.concatenate(down, axis=0)


def stream_kernel(post_ref, low_ref, high_ref, below_ref, above_ref, read_ref):
    row = iota((ZD, NY), 0)
    for i in range(27):
        for x in range(XD):
            v = shifted(post_ref, low_ref, high_ref, i, x)
            if VEL[i][2] == 1:
                at = 4 * UP_Z.index(i) + x
                v = jnp.where(row == 0, below_ref[at : at + 1], pltpu.roll(v, 1, 0))
            elif VEL[i][2] == -1:
                at = 4 * DOWN_Z.index(i) + x
                v = jnp.where(row == ZD - 1, above_ref[at : at + 1], pltpu.roll(v, ZD - 1, 0))
            read_ref[i, x] = v


def unpack_kernel(back_ref, dest_ref, rank_ref, out_ref):
    hot = jnp.where(iota((NB, M), 0) == dest_ref[...], 1.0, 0.0).astype(BF16)
    hi, lo = split(jnp.transpose(back_ref[...])[:24])
    found = dot_nn(hi, hot) + dot_nn(lo, hot)
    chosen = jnp.where(iota((CAP, M), 0) == rank_ref[...], 1.0, 0.0)
    for c in range(3):
        out_ref[c] = jnp.sum(found[8 * c : 8 * c + 8] * chosen, axis=0, keepdims=True)


def call(kernel, outs, *args, cost=2_000_000, name=None):
    return pl.pallas_call(
        kernel,
        out_shape=[jax.ShapeDtypeStruct(s, d) for s, d in outs],
        in_specs=[pl.BlockSpec(memory_space=pltpu.VMEM)] * len(args),
        out_specs=[pl.BlockSpec(memory_space=pltpu.VMEM)] * len(outs),
        compiler_params=pltpu.CompilerParams(vmem_limit_bytes=LIMIT),
        cost_estimate=pl.CostEstimate(flops=cost, bytes_accessed=cost, transcendentals=0),
        name=name,
    )(*args)


def exchange(x):
    out = lax.all_to_all(x.reshape(NB, 1, NY), "blk", split_axis=0, concat_axis=0, tiled=True)
    return out.reshape(NB, NY)


def ring(axis, count, step):
    return [(i, (i + step) % count) for i in range(count)]


def body(populations, destination, base_cell, offsets, target):
    dest = destination.reshape(1, M)
    cell = base_cell.reshape(1, M)
    offs = offsets.reshape(3, 1, M)
    targ = target.reshape(3, 1, M)
    send, rank = call(pack_kernel, [((NB, NY), F32), ((1, M), jnp.int32)], dest, cell, offs, targ, name="pack")
    recv = exchange(send)
    (vel,) = call(velocity_kernel, [((384, NY), BF16)], populations, name="velocity")
    face = (9, ZD, NY)
    post, back, up, down = call(
        force_kernel,
        [((27, XD, ZD, NY), F32), ((NB, NY), F32), (face, F32), (face, F32)],
        recv, vel, populations, name="force",
    )
    low = lax.ppermute(up, "blk", ring("blk", NB, 1))
    high = lax.ppermute(down, "blk", ring("blk", NB, -1))
    reply = exchange(back)
    edge = (36, NY)
    z_up, z_down = call(edge_kernel, [(edge, F32), (edge, F32)], post, low, high, name="edge")
    below = lax.ppermute(z_up, "sub", ring("sub", 4, 1))
    above = lax.ppermute(z_down, "sub", ring("sub", 4, -1))
    (read,) = call(stream_kernel, [((27, XD, ZD, NY), F32)], post, low, high, below, above, name="stream")
    (pulled,) = call(unpack_kernel, [((3, 1, M), F32)], reply, dest, rank, name="unpack")
    return read, pulled.reshape(1, 1, 3, M)


def solution(mesh):
    in_specs = (
        P(None, "blk", "sub", None),
        P("blk", "sub", None, None),
        P("blk", "sub", None),
        P("blk", "sub", None, None),
        P("blk", "sub", None, None),
    )
    out_specs = (P(None, "blk", "sub", None), P("blk", "sub", None, None))
    return jax.shard_map(body, mesh=mesh, in_specs=in_specs, out_specs=out_specs, check_vma=False)
```

time: 217 us -> 62.4 us (0.29)
  the two profiles are of different devices: /device:TPU:1 before, /device:TPU:6 now
where the time goes in v1:
time: 62.4 us; the launch traced here: 62 us
  starting transfers between devices  38.6 us (62%)
  waiting for transfers between devices  14.9 us (24%)
  Pallas kernels  4.58 us (7%)
  local copies, waits for them, and re-layouts  3.08 us (5%)
  between operations  0.74 us (1%)
    all_to_all x2, starting transfers between devices, exchange(): lax.all_to_all(x.reshape(NB, 1, NY), 'blk', split_axis=0, concat_axis=0,...  23.9 us
    all_to_all x2, waiting for transfers between devices, exchange(): lax.all_to_all(x.reshape(NB, 1, NY), 'blk', split_axis=0, concat_axis=0,...  9.92 us
    ppermute x1, starting transfers between devices, body(): high = lax.ppermute(down, 'blk', ring('blk', NB, -1))  6.96 us
    pallas_call x6, Pallas kernels, call(): pl.pallas_call(kernel, out_shape=[jax.ShapeDtypeStruct(s, d) for s, d in...  4.58 us
    ppermute x1, starting transfers between devices, body(): above = lax.ppermute(z_down, 'sub', ring('sub', 4, -1))  3.46 us
    ppermute x1, waiting for transfers between devices, body(): above = lax.ppermute(z_down, 'sub', ring('sub', 4, -1))  3.41 us
    unnamed x12, local copies, waits for them, and re-layouts  3.08 us
    ppermute x1, starting transfers between devices, body(): below = lax.ppermute(z_up, 'sub', ring('sub', 4, 1))  2.39 us
  transfers between devices with their start and end apart: 6, of which 3 were waited for; matrix products, arithmetic and copies ran while one was open for 0% of the time, Pallas kernels for 2%

profile of v1, /device:TPU:6, one launch (start us, length us, event | category | flops | bytes accessed | tf_op | source)
XLA Modules:
  0.0 62.0 jit_solution(8075809095784457379)
XLA Ops:
  0.6 0.0 copy-start.5
  0.6 0.0 copy-start.2
  0.7 0.7 %copy-done.5 = s32[1,1,512]{2,1,0:T(1,128)S(1)} copy-done((s32[1,1,512]{2,1,0:T(1,128)S(1)}, s32[1,1,512]{2,1,0:T(1,128)}, u32[]{:S(2)}) %copy-start.5) | copy-done | bytes 2072
  1.3 0.0 copy-done.2
  1.3 0.0 copy-start.3
  1.3 0.7 %copy-done.3 = f32[1,1,3,512]{3,1,2,0:T(1,128)S(1)} copy-done((f32[1,1,3,512]{3,1,2,0:T(1,128)S(1)}, f32[1,1,3,512]{3,1,2,0:T(1,128)}, u32[]{:S(2)}) %copy-start.3) | copy-done | bytes 6168
  2.0 0.0 copy-start.4
  2.0 0.7 %copy-done.4 = f32[1,1,3,512]{3,1,2,0:T(1,128)S(1)} copy-done((f32[1,1,3,512]{3,1,2,0:T(1,128)S(1)}, f32[1,1,3,512]{3,1,2,0:T(1,128)}, u32[]{:S(2)}) %copy-start.4) | copy-done | bytes 6168
  2.7 1.1 %pack.1 = (f32[128,128]{1,0:T(8,128)}, s32[1,512]{1,0:T(1,128)S(1)}) custom-call(s32[1,512]{1,0:T(1,128)S(1)} %bitcast.17, s32[1,512]{1,0:T(1,128)S(1)} %bitcast.21, f32[3,1,512]{2,1,0:T(1,128)S(1)} %bitcast.19, f32[3,1,512]{2,1,0:T(1,128)S(1)} %bitcast.20), custom_call_target="tpu_custom_call" | custom-call | flops 2000000 | bytes 2000000 | tf_op jit(solution)/shard_map/pack/pallas_call | solution.py:225
  3.9 17.8 %all-to-all-start = ((f32[128,1,128]{2,1,0:T(1,128)}), f32[128,1,128]{2,1,0:T(1,128)S(1)}, u32[]{:S(2)}, u32[]{:S(2)}) async-start(f32[128,1,128]{2,1,0:T(1,128)} %bitcast.5), calls=%async_computation | async-start | bytes 131072 | tf_op jit(solution)/shard_map/all_to_all | solution.py:237
  21.7 0.0 copy-start
  21.7 1.0 %copy-done = f32[27,4,8,128]{3,2,1,0:T(8,128)S(1)} copy-done((f32[27,4,8,128]{3,2,1,0:T(8,128)S(1)}, f32[27,4,8,128]{3,2,1,0:T(8,128)}, u32[]{:S(2)}) %copy-start) | copy-done | bytes 442392
  22.7 0.0 copy-start.1
  22.7 0.1 velocity.1.vel_ref
  22.8 9.9 %all-to-all-done = f32[128,1,128]{2,1,0:T(1,128)S(1)} async-done(((f32[128,1,128]{2,1,0:T(1,128)}), f32[128,1,128]{2,1,0:T(1,128)S(1)}, u32[]{:S(2)}, u32[]{:S(2)}) %all-to-all-start) | async-done | bytes 65568 | tf_op jit(solution)/shard_map/all_to_all | solution.py:237
  32.7 0.0 copy-done.1
  32.7 1.6 %force.1 = (f32[27,4,8,128]{3,2,1,0:T(8,128)S(1)}, f32[128,128]{1,0:T(8,128)}, f32[9,8,128]{2,1,0:T(8,128)S(1)}, f32[9,8,128]{2,1,0:T(8,128)S(1)}) custom-call(f32[128,128]{1,0:T(8,128)S(1)} %bitcast.15, bf16[384,128]{1,0:T(8,128)(2,1)S(1)} %velocity.1.vel_ref, f32[27,4,8,128]{3,2,1,0:T(8,128)S(1)} %copy-done.1), custom_call_target="tpu_custom_call" | custom-call | flops 2000000 | bytes 2000000 | tf_op jit(solution)/shard_map/force/pallas_call | solution.py:225
  34.4 6.1 %all-to-all-start.1 = ((f32[128,1,128]{2,1,0:T(1,128)}), f32[128,1,128]{2,1,0:T(1,128)S(1)}, u32[]{:S(2)}, u32[]{:S(2)}) async-start(f32[128,1,128]{2,1,0:T(1,128)} %bitcast.8), calls=%async_computation.1 | async-start | bytes 131072 | tf_op jit(solution)/shard_map/all_to_all | solution.py:237
  40.5 1.9 %collective-permute-start = (f32[9,8,128]{2,1,0:T(8,128)S(1)}, f32[9,8,128]{2,1,0:T(8,128)S(1)}, u32[]{:S(2)}, u32[]{:S(2)}) collective-permute-start(f32[9,8,128]{2,1,0:T(8,128)S(1)} %get-tuple-element.12), channel_id=1, source_target_pairs={{0,4},{4,8},{8,12},{12,16},{16,20},{20,24},{24,28},{28,32},{32,36}... | collective-permute-start | bytes 110600 | tf_op jit(solution)/shard_map/ppermute | solution.py:259
  42.4 7.0 %collective-permute-start.1 = (f32[9,8,128]{2,1,0:T(8,128)S(1)}, f32[9,8,128]{2,1,0:T(8,128)S(1)}, u32[]{:S(2)}, u32[]{:S(2)}) collective-permute-start(f32[9,8,128]{2,1,0:T(8,128)S(1)} %get-tuple-element.13), channel_id=1, source_target_pairs={{0,508},{4,0},{8,4},{12,8},{16,12},{20,16},{24,20},{28,24},{32,28}... | collective-permute-start | bytes 110600 | tf_op jit(solution)/shard_map/ppermute | solution.py:260
  49.4 0.0 collective-permute-done.low_ref
  49.4 1.6 %collective-permute-done.1.high_ref = f32[9,8,128]{2,1,0:T(8,128)S(1)} collective-permute-done((f32[9,8,128]{2,1,0:T(8,128)S(1)}, f32[9,8,128]{2,1,0:T(8,128)S(1)}, u32[]{:S(2)}, u32[]{:S(2)}) %collective-permute-start.1) | collective-permute-done | bytes 36896 | tf_op jit(solution)/shard_map/ppermute | solution.py:260
  51.0 2.4 %collective-permute-start.2 = (f32[36,128]{1,0:T(8,128)S(1)}, f32[36,128]{1,0:T(8,128)S(1)}, u32[]{:S(2)}, u32[]{:S(2)}) collective-permute-start(f32[36,128]{1,0:T(8,128)S(1)} %get-tuple-element.14), channel_id=1, source_target_pairs={{0,1},{1,2},{2,3},{3,0},{4,5},{5,6},{6,7},{7,4},{8,9},{9,10},{10,1... | collective-permute-start | bytes 55304 | tf_op jit(solution)/shard_map/ppermute | solution.py:264
  53.4 3.5 %collective-permute-start.3 = (f32[36,128]{1,0:T(8,128)S(1)}, f32[36,128]{1,0:T(8,128)S(1)}, u32[]{:S(2)}, u32[]{:S(2)}) collective-permute-start(f32[36,128]{1,0:T(8,128)S(1)} %get-tuple-element.15), channel_id=1, source_target_pairs={{0,3},{1,0},{2,1},{3,2},{4,7},{5,4},{6,5},{7,6},{8,11},{9,8},{10,9... | collective-permute-start | bytes 55304 | tf_op jit(solution)/shard_map/ppermute | solution.py:265
  56.9 0.0 collective-permute-done.2.below_ref
  56.9 3.4 %collective-permute-done.3.above_ref = f32[36,128]{1,0:T(8,128)S(1)} collective-permute-done((f32[36,128]{1,0:T(8,128)S(1)}, f32[36,128]{1,0:T(8,128)S(1)}, u32[]{:S(2)}, u32[]{:S(2)}) %collective-permute-start.3) | collective-permute-done | bytes 18464 | tf_op jit(solution)/shard_map/ppermute | solution.py:265
  60.3 0.8 %stream.1 = f32[27,4,8,128]{3,2,1,0:T(8,128)} custom-call(f32[27,4,8,128]{3,2,1,0:T(8,128)S(1)} %get-tuple-element.11.post_ref, f32[9,8,128]{2,1,0:T(8,128)S(1)} %collective-permute-done.low_ref, f32[9,8,128]{2,1,0:T(8,128)S(1)} %collective-permute-done.1.high_ref, f32[36,128]{1,0:T(8,128)S(1)} %collective-permute-done.2.below_ref, ...), custom_call_target="tpu_custom_call" | custom-call | flops 2000000 | bytes 2000000 | tf_op jit(solution)/shard_map/stream/pallas_call | solution.py:225
  61.1 0.0 all-to-all-done.1
  61.1 0.8 %unpack.1 = f32[3,1,512]{2,1,0:T(1,128)} custom-call(f32[128,128]{1,0:T(8,128)S(1)} %bitcast.16, s32[1,512]{1,0:T(1,128)S(1)} %bitcast.18, s32[1,512]{1,0:T(1,128)S(1)} %get-tuple-element.17.rank_ref), custom_call_target="tpu_custom_call" | custom-call | flops 2000000 | bytes 2000000 | tf_op jit(solution)/shard_map/unpack/pallas_call | solution.py:225
  (1 shorter events, 0.0 us)
Async XLA Ops:
  0.6 0.7 %copy-start.5 = (s32[1,1,512]{2,1,0:T(1,128)S(1)}, s32[1,1,512]{2,1,0:T(1,128)}, u32[]{:S(2)}) copy-start(s32[1,1,512]{2,1,0:T(1,128)} %param.7) | copy-start | bytes 6148
  0.6 0.7 %copy-start.2 = (s32[1,1,512,1]{2,3,1,0:T(1,128)S(1)}, s32[1,1,512,1]{2,3,1,0:T(1,128)}, u32[]{:S(2)}) copy-start(s32[1,1,512,1]{2,3,1,0:T(1,128)} %param.6) | copy-start | bytes 6148
  1.3 0.7 %copy-start.3 = (f32[1,1,3,512]{3,1,2,0:T(1,128)S(1)}, f32[1,1,3,512]{3,1,2,0:T(1,128)}, u32[]{:S(2)}) copy-start(f32[1,1,3,512]{3,1,2,0:T(1,128)} %param.8) | copy-start | bytes 18436
  2.0 0.7 %copy-start.4 = (f32[1,1,3,512]{3,1,2,0:T(1,128)S(1)}, f32[1,1,3,512]{3,1,2,0:T(1,128)}, u32[]{:S(2)}) copy-start(f32[1,1,3,512]{3,1,2,0:T(1,128)} %param.9) | copy-start | bytes 18436
  3.9 28.9 %all-to-all-start = ((f32[128,1,128]{2,1,0:T(1,128)}), f32[128,1,128]{2,1,0:T(1,128)S(1)}, u32[]{:S(2)}, u32[]{:S(2)}) async-start(f32[128,1,128]{2,1,0:T(1,128)} %bitcast.5), calls=%async_computation | async-start | bytes 131072 | tf_op jit(solution)/shard_map/all_to_all | solution.py:237
  21.7 1.0 %copy-start = (f32[27,4,8,128]{3,2,1,0:T(8,128)S(1)}, f32[27,4,8,128]{3,2,1,0:T(8,128)}, u32[]{:S(2)}) copy-start(f32[27,4,8,128]{3,2,1,0:T(8,128)} %pop_ref.3) | copy-start | bytes 1327108
  22.7 10.1 %copy-start.1 = (f32[27,4,8,128]{3,2,1,0:T(8,128)S(1)}, f32[27,4,8,128]{3,2,1,0:T(8,128)}, u32[]{:S(2)}) copy-start(f32[27,4,8,128]{3,2,1,0:T(8,128)} %pop_ref.3) | copy-start | bytes 1327108
  34.4 26.8 %all-to-all-start.1 = ((f32[128,1,128]{2,1,0:T(1,128)}), f32[128,1,128]{2,1,0:T(1,128)S(1)}, u32[]{:S(2)}, u32[]{:S(2)}) async-start(f32[128,1,128]{2,1,0:T(1,128)} %bitcast.8), calls=%async_computation.1 | async-start | bytes 131072 | tf_op jit(solution)/shard_map/all_to_all | solution.py:237
  40.5 8.9 %collective-permute-start = (f32[9,8,128]{2,1,0:T(8,128)S(1)}, f32[9,8,128]{2,1,0:T(8,128)S(1)}, u32[]{:S(2)}, u32[]{:S(2)}) collective-permute-start(f32[9,8,128]{2,1,0:T(8,128)S(1)} %get-tuple-element.12), channel_id=1, source_target_pairs={{0,4},{4,8},{8,12},{12,16},{16,20},{20,24},{24,28},{28,32},{32,36}... | collective-permute-start | bytes 110600 | tf_op jit(solution)/shard_map/ppermute | solution.py:259
  42.4 8.6 %collective-permute-start.1 = (f32[9,8,128]{2,1,0:T(8,128)S(1)}, f32[9,8,128]{2,1,0:T(8,128)S(1)}, u32[]{:S(2)}, u32[]{:S(2)}) collective-permute-start(f32[9,8,128]{2,1,0:T(8,128)S(1)} %get-tuple-element.13), channel_id=1, source_target_pairs={{0,508},{4,0},{8,4},{12,8},{16,12},{20,16},{24,20},{28,24},{32,28}... | collective-permute-start | bytes 110600 | tf_op jit(solution)/shard_map/ppermute | solution.py:260
  51.0 5.9 %collective-permute-start.2 = (f32[36,128]{1,0:T(8,128)S(1)}, f32[36,128]{1,0:T(8,128)S(1)}, u32[]{:S(2)}, u32[]{:S(2)}) collective-permute-start(f32[36,128]{1,0:T(8,128)S(1)} %get-tuple-element.14), channel_id=1, source_target_pairs={{0,1},{1,2},{2,3},{3,0},{4,5},{5,6},{6,7},{7,4},{8,9},{9,10},{10,1... | collective-permute-start | bytes 55304 | tf_op jit(solution)/shard_map/ppermute | solution.py:264
  53.4 6.9 %collective-permute-start.3 = (f32[36,128]{1,0:T(8,128)S(1)}, f32[36,128]{1,0:T(8,128)S(1)}, u32[]{:S(2)}, u32[]{:S(2)}) collective-permute-start(f32[36,128]{1,0:T(8,128)S(1)} %get-tuple-element.15), channel_id=1, source_target_pairs={{0,3},{1,0},{2,1},{3,2},{4,7},{5,4},{6,5},{7,6},{8,11},{9,8},{10,9... | collective-permute-start | bytes 55304 | tf_op jit(solution)/shard_map/ppermute | solution.py:265

commit v2 on v1

--- a/solution.py
+++ b/solution.py
@@ -21,6 +21,8 @@
 UP_Z = [i for i in range(27) if VEL[i][2] == 1]
 DOWN_Z = [i for i in range(27) if VEL[i][2] == -1]
 LIMIT = 12 * 1024 * 1024
+FIRST = 56 * 1024 * 1024
+LATE = True
 
 
 def iota(shape, dim):
@@ -97,7 +99,8 @@
     return total
 
 
-def force_kernel(recv_ref, vel_ref, pop_ref, post_ref, back_ref, up_ref, down_ref):
+def force_kernel(recv_ref, vel_ref, pop_ref, post_ref, back_ref, pair_ref, cross_ref):
+    first = (lax.axis_index("blk") & 1) == 0
     table = jnp.transpose(recv_ref[...])
     feat = [table[8 * k : 8 * k + 8] for k in range(8)]
     ox, oy, oz = feat[0], feat[1], feat[2]
@@ -171,44 +174,53 @@
                 if VEL[k][1]:
                     out = pltpu.roll(out, VEL[k][1] % NY, 1)
                 post_ref[k, x] = out
-                if x == XD - 1 and VEL[k][0] == 1:
-                    up_ref[UP_X.index(k)] = out
-                if x == 0 and VEL[k][0] == -1:
-                    down_ref[DOWN_X.index(k)] = out
-
-
-def shifted(post_ref, low_ref, high_ref, i, x):
+
+
+    for k in range(9):
+        up, down = post_ref[UP_X[k], XD - 1], post_ref[DOWN_X[k], 0]
+        pair_ref[k] = jnp.where(first, up, down)
+        cross_ref[k] = jnp.where(first, down, up)
+
+
+def shifted(even, post_ref, pair_ref, cross_ref, i, x):
     at = x - VEL[i][0]
     if at < 0:
-        return low_ref[UP_X.index(i)]
+        k = UP_X.index(i)
+        return jnp.where(even, cross_ref[k], pair_ref[k])
     if at >= XD:
-        return high_ref[DOWN_X.index(i)]
+        k = DOWN_X.index(i)
+        return jnp.where(even, pair_ref[k], cross_ref[k])
     return post_ref[i, at]
 
 
-def edge_kernel(post_ref, low_ref, high_ref, up_ref, down_ref):
+def edge_kernel(post_ref, low_ref, high_ref, pair_ref, cross_ref):
+    even, even_z = (lax.axis_index("blk") & 1) == 0, (lax.axis_index("sub") & 1) == 0
     up, down = [], []
     for i in UP_Z:
         for x in range(XD):
-            up.append(shifted(post_ref, low_ref, high_ref, i, x)[ZD - 1 :])
+            up.append(shifted(even, post_ref, low_ref, high_ref, i, x)[ZD - 1 :])
     for i in DOWN_Z:
         for x in range(XD):
-            down.append(shifted(post_ref, low_ref, high_ref, i, x)[:1])
-    up_ref[...] = jnp.concatenate(up, axis=0)
-    down_ref[...] = jnp.concatenate(down, axis=0)
-
-
-def stream_kernel(post_ref, low_ref, high_ref, below_ref, above_ref, read_ref):
+            down.append(shifted(even, post_ref, low_ref, high_ref, i, x)[:1])
+    up, down = jnp.concatenate(up, axis=0), jnp.concatenate(down, axis=0)
+    pair_ref[...] = jnp.where(even_z, up, down)
+    cross_ref[...] = jnp.where(even_z, down, up)
+
+
+def stream_kernel(post_ref, low_ref, high_ref, near_ref, far_ref, read_ref):
+    even, even_z = (lax.axis_index("blk") & 1) == 0, (lax.axis_index("sub") & 1) == 0
     row = iota((ZD, NY), 0)
+    near, far = near_ref[...], far_ref[...]
+    below, above = jnp.where(even_z, far, near), jnp.where(even_z, near, far)
     for i in range(27):
         for x in range(XD):
-            v = shifted(post_ref, low_ref, high_ref, i, x)
+            v = shifted(even, post_ref, low_ref, high_ref, i, x)
             if VEL[i][2] == 1:
                 at = 4 * UP_Z.index(i) + x
-                v = jnp.where(row == 0, below_ref[at : at + 1], pltpu.roll(v, 1, 0))
+                v = jnp.where(row == 0, below[at : at + 1], pltpu.roll(v, 1, 0))
             elif VEL[i][2] == -1:
                 at = 4 * DOWN_Z.index(i) + x
-                v = jnp.where(row == ZD - 1, above_ref[at : at + 1], pltpu.roll(v, ZD - 1, 0))
+                v = jnp.where(row == ZD - 1, above[at : at + 1], pltpu.roll(v, ZD - 1, 0))
             read_ref[i, x] = v
 
 
@@ -221,13 +233,13 @@
         out_ref[c] = jnp.sum(found[8 * c : 8 * c + 8] * chosen, axis=0, keepdims=True)
 
 
-def call(kernel, outs, *args, cost=2_000_000, name=None):
+def call(kernel, outs, *args, cost=2_000_000, name=None, limit=LIMIT):
     return pl.pallas_call(
         kernel,
         out_shape=[jax.ShapeDtypeStruct(s, d) for s, d in outs],
         in_specs=[pl.BlockSpec(memory_space=pltpu.VMEM)] * len(args),
         out_specs=[pl.BlockSpec(memory_space=pltpu.VMEM)] * len(outs),
-        compiler_params=pltpu.CompilerParams(vmem_limit_bytes=LIMIT),
+        compiler_params=pltpu.CompilerParams(vmem_limit_bytes=limit),
         cost_estimate=pl.CostEstimate(flops=cost, bytes_accessed=cost, transcendentals=0),
         name=name,
     )(*args)
@@ -238,8 +250,9 @@
     return out.reshape(NB, NY)
 
 
-def ring(axis, count, step):
-    return [(i, (i + step) % count) for i in range(count)]
+def swaps(count, first):
+    ends = [(k % count, (k + 1) % count) for k in range(first, count + first, 2)]
+    return ends + [(b, a) for a, b in ends]
 
 
 def body(populations, destination, base_cell, offsets, target):
@@ -247,24 +260,26 @@
     cell = base_cell.reshape(1, M)
     offs = offsets.reshape(3, 1, M)
     targ = target.reshape(3, 1, M)
-    send, rank = call(pack_kernel, [((NB, NY), F32), ((1, M), jnp.int32)], dest, cell, offs, targ, name="pack")
+    send, rank = call(pack_kernel, [((NB, NY), F32), ((1, M), jnp.int32)], dest, cell, offs, targ, name="pack", limit=FIRST)
     recv = exchange(send)
     (vel,) = call(velocity_kernel, [((384, NY), BF16)], populations, name="velocity")
     face = (9, ZD, NY)
-    post, back, up, down = call(
+    post, back, pair, cross = call(
         force_kernel,
         [((27, XD, ZD, NY), F32), ((NB, NY), F32), (face, F32), (face, F32)],
         recv, vel, populations, name="force",
     )
-    low = lax.ppermute(up, "blk", ring("blk", NB, 1))
-    high = lax.ppermute(down, "blk", ring("blk", NB, -1))
     reply = exchange(back)
+    pair = lax.ppermute(pair, "blk", swaps(NB, 0))
+    cross = lax.ppermute(cross, "blk", swaps(NB, 1))
     edge = (36, NY)
-    z_up, z_down = call(edge_kernel, [(edge, F32), (edge, F32)], post, low, high, name="edge")
-    below = lax.ppermute(z_up, "sub", ring("sub", 4, 1))
-    above = lax.ppermute(z_down, "sub", ring("sub", 4, -1))
-    (read,) = call(stream_kernel, [((27, XD, ZD, NY), F32)], post, low, high, below, above, name="stream")
+    near, far = call(edge_kernel, [(edge, F32), (edge, F32)], post, pair, cross, name="edge")
+    near = lax.ppermute(near, "sub", swaps(4, 0))
+    far = lax.ppermute(far, "sub", swaps(4, 1))
     (pulled,) = call(unpack_kernel, [((3, 1, M), F32)], reply, dest, rank, name="unpack")
+    if LATE:
+        near, far, pulled = lax.optimization_barrier((near, far, pulled))
+    (read,) = call(stream_kernel, [((27, XD, ZD, NY), F32)], post, pair, cross, near, far, name="stream")
     return read, pulled.reshape(1, 1, 3, M)
 
 

time: 62.4 us -> 61.1 us (0.979)
  local copies, waits for them, and re-layouts: 3.08 us -> 1.02 us
  Pallas kernels: 4.58 us -> 5.55 us
    unnamed x12 -> x8, local copies, waits for them, and re-layouts: 3.08 us -> 1.02 us
    pallas_call x6, Pallas kernels: 4.58 us -> 5.55 us  [call(): pl.pallas_call(kernel, out_shape=[jax.ShapeDtypeStruct(s, d) for s, d in...]
where the time goes in v2:
time: 61.1 us; the launch traced here: 60.7 us
  starting transfers between devices  38.9 us (64%)
  waiting for transfers between devices  14.5 us (24%)
  Pallas kernels  5.55 us (9%)
  local copies, waits for them, and re-layouts  1.02 us (2%)
  between operations  0.75 us (1%)
    all_to_all x2, starting transfers between devices, exchange(): lax.all_to_all(x.reshape(NB, 1, NY), 'blk', split_axis=0, concat_axis=0,...  24 us
    all_to_all x2, waiting for transfers between devices, exchange(): lax.all_to_all(x.reshape(NB, 1, NY), 'blk', split_axis=0, concat_axis=0,...  9.92 us
    ppermute x1, starting transfers between devices, body(): cross = lax.ppermute(cross, 'blk', swaps(NB, 1))  7.21 us
    pallas_call x6, Pallas kernels, call(): pl.pallas_call(kernel, out_shape=[jax.ShapeDtypeStruct(s, d) for s, d in...  5.55 us
    ppermute x1, starting transfers between devices, body(): far = lax.ppermute(far, 'sub', swaps(4, 1))  3.05 us
    ppermute x1, waiting for transfers between devices, body(): far = lax.ppermute(far, 'sub', swaps(4, 1))  2.96 us
    ppermute x1, starting transfers between devices, body(): near = lax.ppermute(near, 'sub', swaps(4, 0))  2.74 us
    ppermute x1, starting transfers between devices, body(): pair = lax.ppermute(pair, 'blk', swaps(NB, 0))  1.92 us
  transfers between devices with their start and end apart: 6, of which 3 were waited for; matrix products, arithmetic and copies ran while one was open for 0% of the time, Pallas kernels for 2%

profile of v2, /device:TPU:6, one launch (start us, length us, event | category | flops | bytes accessed | tf_op | source)
XLA Modules:
  0.0 60.7 jit_solution(14434439361471478452)
XLA Ops:
  0.6 1.9 %pack.1 = (f32[128,128]{1,0:T(8,128)}, s32[1,512]{1,0:T(1,128)}) custom-call(s32[1,512]{1,0:T(1,128)} %bitcast.17, s32[1,512]{1,0:T(1,128)} %bitcast.23, f32[3,1,512]{2,1,0:T(1,128)} %bitcast.21, f32[3,1,512]{2,1,0:T(1,128)} %bitcast.22), custom_call_target="tpu_custom_call" | custom-call | flops 2000000 | bytes 2000000 | tf_op jit(solution)/shard_map/pack/pallas_call | solution.py:237
  2.5 17.8 %all-to-all-start = ((f32[128,1,128]{2,1,0:T(1,128)}), f32[128,1,128]{2,1,0:T(1,128)S(1)}, u32[]{:S(2)}, u32[]{:S(2)}) async-start(f32[128,1,128]{2,1,0:T(1,128)} %bitcast.19), calls=%async_computation | async-start | bytes 131072 | tf_op jit(solution)/shard_map/all_to_all | solution.py:249
  20.3 0.0 copy-start
  20.3 1.0 %copy-done = f32[27,4,8,128]{3,2,1,0:T(8,128)S(1)} copy-done((f32[27,4,8,128]{3,2,1,0:T(8,128)S(1)}, f32[27,4,8,128]{3,2,1,0:T(8,128)}, u32[]{:S(2)}) %copy-start) | copy-done | bytes 442392
  21.4 0.0 copy-start.1
  21.4 0.1 velocity.1.vel_ref
  21.5 9.9 %all-to-all-done = f32[128,1,128]{2,1,0:T(1,128)S(1)} async-done(((f32[128,1,128]{2,1,0:T(1,128)}), f32[128,1,128]{2,1,0:T(1,128)S(1)}, u32[]{:S(2)}, u32[]{:S(2)}) %all-to-all-start) | async-done | bytes 65568 | tf_op jit(solution)/shard_map/all_to_all | solution.py:249
  31.4 0.0 copy-done.1
  31.4 1.9 %force.1 = (f32[27,4,8,128]{3,2,1,0:T(8,128)S(1)}, f32[128,128]{1,0:T(8,128)}, f32[9,8,128]{2,1,0:T(8,128)S(1)}, f32[9,8,128]{2,1,0:T(8,128)S(1)}) custom-call(f32[128,128]{1,0:T(8,128)S(1)} %bitcast.15, bf16[384,128]{1,0:T(8,128)(2,1)S(1)} %velocity.1.vel_ref, f32[27,4,8,128]{3,2,1,0:T(8,128)S(1)} %copy-done.1), custom_call_target="tpu_custom_call" | custom-call | flops 2000000 | bytes 2000000 | tf_op jit(solution)/shard_map/force/pallas_call | solution.py:237
  33.3 6.1 %all-to-all-start.1 = ((f32[128,1,128]{2,1,0:T(1,128)}), f32[128,1,128]{2,1,0:T(1,128)S(1)}, u32[]{:S(2)}, u32[]{:S(2)}) async-start(f32[128,1,128]{2,1,0:T(1,128)} %bitcast.8), calls=%async_computation.1 | async-start | bytes 131072 | tf_op jit(solution)/shard_map/all_to_all | solution.py:249
  39.4 1.9 %collective-permute-start = (f32[9,8,128]{2,1,0:T(8,128)S(1)}, f32[9,8,128]{2,1,0:T(8,128)S(1)}, u32[]{:S(2)}, u32[]{:S(2)}) collective-permute-start(f32[9,8,128]{2,1,0:T(8,128)S(1)} %get-tuple-element.15), channel_id=1, source_target_pairs={{0,4},{8,12},{16,20},{24,28},{32,36},{40,44},{48,52},{56,60},{64,6... | collective-permute-start | bytes 110600 | tf_op jit(solution)/shard_map/ppermute | solution.py:273
  41.4 7.2 %collective-permute-start.1 = (f32[9,8,128]{2,1,0:T(8,128)S(1)}, f32[9,8,128]{2,1,0:T(8,128)S(1)}, u32[]{:S(2)}, u32[]{:S(2)}) collective-permute-start(f32[9,8,128]{2,1,0:T(8,128)S(1)} %get-tuple-element.16), channel_id=1, source_target_pairs={{4,8},{12,16},{20,24},{28,32},{36,40},{44,48},{52,56},{60,64},{68,... | collective-permute-start | bytes 110600 | tf_op jit(solution)/shard_map/ppermute | solution.py:274
  48.6 0.0 collective-permute-done.low_ref
  48.6 1.6 %collective-permute-done.1.high_ref = f32[9,8,128]{2,1,0:T(8,128)S(1)} collective-permute-done((f32[9,8,128]{2,1,0:T(8,128)S(1)}, f32[9,8,128]{2,1,0:T(8,128)S(1)}, u32[]{:S(2)}, u32[]{:S(2)}) %collective-permute-start.1) | collective-permute-done | bytes 36896 | tf_op jit(solution)/shard_map/ppermute | solution.py:274
  50.2 2.7 %collective-permute-start.2 = (f32[36,128]{1,0:T(8,128)S(1)}, f32[36,128]{1,0:T(8,128)S(1)}, u32[]{:S(2)}, u32[]{:S(2)}) collective-permute-start(f32[36,128]{1,0:T(8,128)S(1)} %get-tuple-element.17), channel_id=1, source_target_pairs={{0,1},{2,3},{1,0},{3,2},{4,5},{6,7},{5,4},{7,6},{8,9},{10,11},{9,8... | collective-permute-start | bytes 55304 | tf_op jit(solution)/shard_map/ppermute | solution.py:277
  53.0 0.0 copy-start.3
  53.0 0.0 copy-start.2
  53.0 3.1 %collective-permute-start.3 = (f32[36,128]{1,0:T(8,128)S(1)}, f32[36,128]{1,0:T(8,128)S(1)}, u32[]{:S(2)}, u32[]{:S(2)}) collective-permute-start(f32[36,128]{1,0:T(8,128)S(1)} %get-tuple-element.18), channel_id=1, source_target_pairs={{1,2},{3,0},{2,1},{0,3},{5,6},{7,4},{6,5},{4,7},{9,10},{11,8},{10,... | collective-permute-start | bytes 55304 | tf_op jit(solution)/shard_map/ppermute | solution.py:278
  56.1 0.0 all-to-all-done.1
  56.1 0.0 copy-done.3
  56.1 0.0 copy-done.2
  56.1 0.8 %unpack.1 = f32[3,1,512]{2,1,0:T(1,128)} custom-call(f32[128,128]{1,0:T(8,128)S(1)} %bitcast.16, s32[1,512]{1,0:T(1,128)S(1)} %bitcast.18, s32[1,512]{1,0:T(1,128)S(1)} %copy-done.3), custom_call_target="tpu_custom_call" | custom-call | flops 2000000 | bytes 2000000 | tf_op jit(solution)/shard_map/unpack/pallas_call | solution.py:237
  56.9 0.0 collective-permute-done.2.near_ref
  56.9 3.0 %collective-permute-done.3.far_ref = f32[36,128]{1,0:T(8,128)S(1)} collective-permute-done((f32[36,128]{1,0:T(8,128)S(1)}, f32[36,128]{1,0:T(8,128)S(1)}, u32[]{:S(2)}, u32[]{:S(2)}) %collective-permute-start.3) | collective-permute-done | bytes 18464 | tf_op jit(solution)/shard_map/ppermute | solution.py:278
  59.9 0.8 %stream.1 = f32[27,4,8,128]{3,2,1,0:T(8,128)} custom-call(f32[27,4,8,128]{3,2,1,0:T(8,128)S(1)} %get-tuple-element.14.post_ref, f32[9,8,128]{2,1,0:T(8,128)S(1)} %collective-permute-done.low_ref, f32[9,8,128]{2,1,0:T(8,128)S(1)} %collective-permute-done.1.high_ref, f32[36,128]{1,0:T(8,128)S(1)} %collective-permute-done.2.near_ref, ...), custom_call_target="tpu_custom_call" | custom-call | flops 2000000 | bytes 2000000 | tf_op jit(solution)/shard_map/stream/pallas_call | solution.py:237
  (1 shorter events, 0.0 us)
Async XLA Ops:
  2.5 28.9 %all-to-all-start = ((f32[128,1,128]{2,1,0:T(1,128)}), f32[128,1,128]{2,1,0:T(1,128)S(1)}, u32[]{:S(2)}, u32[]{:S(2)}) async-start(f32[128,1,128]{2,1,0:T(1,128)} %bitcast.19), calls=%async_computation | async-start | bytes 131072 | tf_op jit(solution)/shard_map/all_to_all | solution.py:249
  20.3 1.0 %copy-start = (f32[27,4,8,128]{3,2,1,0:T(8,128)S(1)}, f32[27,4,8,128]{3,2,1,0:T(8,128)}, u32[]{:S(2)}) copy-start(f32[27,4,8,128]{3,2,1,0:T(8,128)} %pop_ref.3) | copy-start | bytes 1327108
  21.4 10.1 %copy-start.1 = (f32[27,4,8,128]{3,2,1,0:T(8,128)S(1)}, f32[27,4,8,128]{3,2,1,0:T(8,128)}, u32[]{:S(2)}) copy-start(f32[27,4,8,128]{3,2,1,0:T(8,128)} %pop_ref.3) | copy-start | bytes 1327108
  33.3 22.8 %all-to-all-start.1 = ((f32[128,1,128]{2,1,0:T(1,128)}), f32[128,1,128]{2,1,0:T(1,128)S(1)}, u32[]{:S(2)}, u32[]{:S(2)}) async-start(f32[128,1,128]{2,1,0:T(1,128)} %bitcast.8), calls=%async_computation.1 | async-start | bytes 131072 | tf_op jit(solution)/shard_map/all_to_all | solution.py:249
  39.4 9.1 %collective-permute-start = (f32[9,8,128]{2,1,0:T(8,128)S(1)}, f32[9,8,128]{2,1,0:T(8,128)S(1)}, u32[]{:S(2)}, u32[]{:S(2)}) collective-permute-start(f32[9,8,128]{2,1,0:T(8,128)S(1)} %get-tuple-element.15), channel_id=1, source_target_pairs={{0,4},{8,12},{16,20},{24,28},{32,36},{40,44},{48,52},{56,60},{64,6... | collective-permute-start | bytes 110600 | tf_op jit(solution)/shard_map/ppermute | solution.py:273
  41.4 8.9 %collective-permute-start.1 = (f32[9,8,128]{2,1,0:T(8,128)S(1)}, f32[9,8,128]{2,1,0:T(8,128)S(1)}, u32[]{:S(2)}, u32[]{:S(2)}) collective-permute-start(f32[9,8,128]{2,1,0:T(8,128)S(1)} %get-tuple-element.16), channel_id=1, source_target_pairs={{4,8},{12,16},{20,24},{28,32},{36,40},{44,48},{52,56},{60,64},{68,... | collective-permute-start | bytes 110600 | tf_op jit(solution)/shard_map/ppermute | solution.py:274
  50.2 6.7 %collective-permute-start.2 = (f32[36,128]{1,0:T(8,128)S(1)}, f32[36,128]{1,0:T(8,128)S(1)}, u32[]{:S(2)}, u32[]{:S(2)}) collective-permute-start(f32[36,128]{1,0:T(8,128)S(1)} %get-tuple-element.17), channel_id=1, source_target_pairs={{0,1},{2,3},{1,0},{3,2},{4,5},{6,7},{5,4},{7,6},{8,9},{10,11},{9,8... | collective-permute-start | bytes 55304 | tf_op jit(solution)/shard_map/ppermute | solution.py:277
  53.0 3.1 %copy-start.3 = (s32[1,512]{1,0:T(1,128)S(1)}, s32[1,512]{1,0:T(1,128)}, u32[]{:S(2)}) copy-start(s32[1,512]{1,0:T(1,128)} %get-tuple-element.20.rank_ref) | copy-start | bytes 6148
  53.0 3.1 %copy-start.2 = (s32[1,1,512,1]{2,3,1,0:T(1,128)S(1)}, s32[1,1,512,1]{2,3,1,0:T(1,128)}, u32[]{:S(2)}) copy-start(s32[1,1,512,1]{2,3,1,0:T(1,128)} %param.6) | copy-start | bytes 6148
  53.0 6.9 %collective-permute-start.3 = (f32[36,128]{1,0:T(8,128)S(1)}, f32[36,128]{1,0:T(8,128)S(1)}, u32[]{:S(2)}, u32[]{:S(2)}) collective-permute-start(f32[36,128]{1,0:T(8,128)S(1)} %get-tuple-element.18), channel_id=1, source_target_pairs={{1,2},{3,0},{2,1},{0,3},{5,6},{7,4},{6,5},{4,7},{9,10},{11,8},{10,... | collective-permute-start | bytes 55304 | tf_op jit(solution)/shard_map/ppermute | solution.py:278

commit v3 on v2

--- a/solution.py
+++ b/solution.py
@@ -22,7 +22,8 @@
 DOWN_Z = [i for i in range(27) if VEL[i][2] == -1]
 LIMIT = 12 * 1024 * 1024
 FIRST = 56 * 1024 * 1024
-LATE = True
+TURN = 112
+EDGE = 2_000_000_000
 
 
 def iota(shape, dim):
@@ -42,21 +43,28 @@
     return lax.dot_general(a, b, (((1,), (0,)), ((), ())), preferred_element_type=F32)
 
 
-def pack_kernel(dest_ref, cell_ref, offs_ref, targ_ref, send_ref, rank_ref):
-    owner = dest_ref[...]
+def pack_kernel(dest_ref, cell_ref, offs_ref, targ_ref, send_ref, row_ref, rank_ref):
+    owner = (dest_ref[...] - TURN) & (NB - 1)
+    row_ref[...] = owner
     hot = jnp.where(iota((NB, M), 0) == owner, 1.0, 0.0)
     hot16 = hot.astype(BF16)
-    before = jnp.where(iota((M, M), 0) < iota((M, M), 1), 1.0, 0.0).astype(BF16)
-    count = dot_nn(hot16, before)
-    rank = jnp.sum(count * hot, axis=0, keepdims=True).astype(jnp.int32)
+    blocks = [slice(NB * k, NB * k + NB) for k in range(M // NB)]
+    column = iota((NB, 2 * NB), 1)
+    before = jnp.where((iota((NB, 2 * NB), 0) < column) | (column >= NB), 1.0, 0.0).astype(BF16)
+    count = dot_nn(jnp.concatenate([hot16[:, k] for k in blocks], axis=0), before)
+    ranks, passed = [], 0.0
+    for k in blocks:
+        ranks.append(jnp.sum((count[k, :NB] + passed) * hot[:, k], axis=0, keepdims=True))
+        passed = passed + count[k, NB:]
+    rank = jnp.concatenate(ranks, axis=1).astype(jnp.int32)
     rank_ref[...] = rank
     chosen = jnp.where(iota((CAP, M), 0) == rank, 1.0, 0.0)
     feats = [offs_ref[k] for k in range(3)] + [targ_ref[k] for k in range(3)]
     feats += [cell_ref[...].astype(F32), jnp.ones((1, M), F32)]
     table = jnp.concatenate([chosen * f for f in feats], axis=0)
     hi, lo = split(table)
-    packed = dot_nt(hot16, hi) + dot_nt(hot16, lo)
-    send_ref[...] = jnp.concatenate([packed, jnp.zeros((NB, 64), F32)], axis=1)
+    packed = dot_nt(hot16, jnp.concatenate([hi, lo], axis=0))
+    send_ref[...] = packed + pltpu.roll(packed, 64, 1)
 
 
 def moments(load):
@@ -78,7 +86,9 @@
     return rho, jx, jy, jz
 
 
-def velocity_kernel(pop_ref, vel_ref):
+def velocity_kernel(pop_ref, row_in, rank_in, vel_ref, row_ref, rank_ref):
+    row_ref[...] = row_in[...]
+    rank_ref[...] = rank_in[...]
     comps = [[], [], []]
     for x in range(XD):
         rho, jx, jy, jz = moments(lambda i: pop_ref[i, x])
@@ -99,7 +109,7 @@
     return total
 
 
-def force_kernel(recv_ref, vel_ref, pop_ref, post_ref, back_ref, pair_ref, cross_ref):
+def force_kernel(recv_ref, vel_ref, pop_ref, post_ref, back_hbm, pair_ref, cross_ref, back_ref, sem):
     first = (lax.axis_index("blk") & 1) == 0
     table = jnp.transpose(recv_ref[...])
     feat = [table[8 * k : 8 * k + 8] for k in range(8)]
@@ -146,6 +156,8 @@
         far.append(jnp.concatenate(col1, axis=0))
     reply = jnp.concatenate([p for comp in pulls for p in comp] + [jnp.zeros((NB - 24, NB), F32)], axis=0)
     back_ref[...] = jnp.transpose(reply)
+    sent = pltpu.make_async_copy(back_ref, back_hbm, sem)
+    sent.start()
     amount = jnp.concatenate([jnp.concatenate(near, axis=1), jnp.concatenate(far, axis=1)], axis=0)
     hi, lo = split(amount)
     field = dot_nt(hi, hot) + dot_nt(lo, hot)
@@ -180,6 +192,7 @@
         up, down = post_ref[UP_X[k], XD - 1], post_ref[DOWN_X[k], 0]
         pair_ref[k] = jnp.where(first, up, down)
         cross_ref[k] = jnp.where(first, down, up)
+    sent.wait()
 
 
 def shifted(even, post_ref, pair_ref, cross_ref, i, x):
@@ -193,7 +206,7 @@
     return post_ref[i, at]
 
 
-def edge_kernel(post_ref, low_ref, high_ref, pair_ref, cross_ref):
+def edge_kernel(post_ref, high_ref, low_ref, pair_ref, cross_ref):
     even, even_z = (lax.axis_index("blk") & 1) == 0, (lax.axis_index("sub") & 1) == 0
     up, down = [], []
     for i in UP_Z:
@@ -207,11 +220,12 @@
     cross_ref[...] = jnp.where(even_z, down, up)
 
 
-def stream_kernel(post_ref, low_ref, high_ref, near_ref, far_ref, read_ref):
+def last_kernel(post_ref, low_ref, high_ref, near_ref, far_ref, back_ref, row_ref, rank_ref, read_hbm, out_ref, read_ref, sems):
     even, even_z = (lax.axis_index("blk") & 1) == 0, (lax.axis_index("sub") & 1) == 0
     row = iota((ZD, NY), 0)
     near, far = near_ref[...], far_ref[...]
     below, above = jnp.where(even_z, far, near), jnp.where(even_z, near, far)
+    copies = []
     for i in range(27):
         for x in range(XD):
             v = shifted(even, post_ref, low_ref, high_ref, i, x)
@@ -222,23 +236,28 @@
                 at = 4 * DOWN_Z.index(i) + x
                 v = jnp.where(row == ZD - 1, above[at : at + 1], pltpu.roll(v, ZD - 1, 0))
             read_ref[i, x] = v
-
-
-def unpack_kernel(back_ref, dest_ref, rank_ref, out_ref):
-    hot = jnp.where(iota((NB, M), 0) == dest_ref[...], 1.0, 0.0).astype(BF16)
+        if i % 9 == 8:
+            part = pl.ds(i - 8, 9)
+            copies.append(pltpu.make_async_copy(read_ref.at[part], read_hbm.at[part], sems.at[i // 9]))
+            copies[-1].start()
+    hot = jnp.where(iota((NB, M), 0) == row_ref[...], 1.0, 0.0).astype(BF16)
     hi, lo = split(jnp.transpose(back_ref[...])[:24])
-    found = dot_nn(hi, hot) + dot_nn(lo, hot)
+    found = dot_nn(jnp.concatenate([hi, lo], axis=0), hot)
+    found = found[:24] + found[24:]
     chosen = jnp.where(iota((CAP, M), 0) == rank_ref[...], 1.0, 0.0)
     for c in range(3):
         out_ref[c] = jnp.sum(found[8 * c : 8 * c + 8] * chosen, axis=0, keepdims=True)
-
-
-def call(kernel, outs, *args, cost=2_000_000, name=None, limit=LIMIT):
+    for copy in copies:
+        copy.wait()
+
+
+def call(kernel, outs, *args, cost=2_000_000, name=None, limit=LIMIT, far=(), scratch=()):
     return pl.pallas_call(
         kernel,
         out_shape=[jax.ShapeDtypeStruct(s, d) for s, d in outs],
         in_specs=[pl.BlockSpec(memory_space=pltpu.VMEM)] * len(args),
-        out_specs=[pl.BlockSpec(memory_space=pltpu.VMEM)] * len(outs),
+        out_specs=[pl.BlockSpec(memory_space=pltpu.HBM if k in far else pltpu.VMEM) for k in range(len(outs))],
+        scratch_shapes=list(scratch),
         compiler_params=pltpu.CompilerParams(vmem_limit_bytes=limit),
         cost_estimate=pl.CostEstimate(flops=cost, bytes_accessed=cost, transcendentals=0),
         name=name,
@@ -246,7 +265,8 @@
 
 
 def exchange(x):
-    out = lax.all_to_all(x.reshape(NB, 1, NY), "blk", split_axis=0, concat_axis=0, tiled=True)
+    order = [(k + TURN) % NB for k in range(NB)]
+    out = lax.all_to_all(x.reshape(NB, 1, NY), "blk", split_axis=0, concat_axis=0, tiled=True, axis_index_groups=[order])
     return out.reshape(NB, NY)
 
 
@@ -260,26 +280,30 @@
     cell = base_cell.reshape(1, M)
     offs = offsets.reshape(3, 1, M)
     targ = target.reshape(3, 1, M)
-    send, rank = call(pack_kernel, [((NB, NY), F32), ((1, M), jnp.int32)], dest, cell, offs, targ, name="pack", limit=FIRST)
+    send, row, rank = call(pack_kernel, [((NB, NY), F32), ((1, M), jnp.int32), ((1, M), jnp.int32)], dest, cell, offs, targ, name="pack", limit=FIRST)
     recv = exchange(send)
-    (vel,) = call(velocity_kernel, [((384, NY), BF16)], populations, name="velocity")
+    ints = ((1, M), jnp.int32)
+    vel, row, rank = call(velocity_kernel, [((384, NY), BF16), ints, ints], populations, row, rank, name="velocity")
     face = (9, ZD, NY)
     post, back, pair, cross = call(
         force_kernel,
         [((27, XD, ZD, NY), F32), ((NB, NY), F32), (face, F32), (face, F32)],
-        recv, vel, populations, name="force",
+        recv, vel, populations, name="force", far=(1,),
+        scratch=[pltpu.VMEM((NB, NY), F32), pltpu.SemaphoreType.DMA],
     )
     reply = exchange(back)
+    cross = lax.ppermute(cross, "blk", swaps(NB, 1))
     pair = lax.ppermute(pair, "blk", swaps(NB, 0))
-    cross = lax.ppermute(cross, "blk", swaps(NB, 1))
     edge = (36, NY)
-    near, far = call(edge_kernel, [(edge, F32), (edge, F32)], post, pair, cross, name="edge")
+    near, far = call(edge_kernel, [(edge, F32), (edge, F32)], post, cross, pair, name="edge", cost=EDGE)
     near = lax.ppermute(near, "sub", swaps(4, 0))
     far = lax.ppermute(far, "sub", swaps(4, 1))
-    (pulled,) = call(unpack_kernel, [((3, 1, M), F32)], reply, dest, rank, name="unpack")
-    if LATE:
-        near, far, pulled = lax.optimization_barrier((near, far, pulled))
-    (read,) = call(stream_kernel, [((27, XD, ZD, NY), F32)], post, pair, cross, near, far, name="stream")
+    whole = (27, XD, ZD, NY)
+    read, pulled = call(
+        last_kernel, [(whole, F32), ((3, 1, M), F32)],
+        post, pair, cross, near, far, reply, row, rank, name="last", far=(0,),
+        scratch=[pltpu.VMEM(whole, F32), pltpu.SemaphoreType.DMA((3,))],
+    )
     return read, pulled.reshape(1, 1, 3, M)
 
 

time: 61.1 us -> 58.5 us (0.957)
  the two profiles are of different devices: /device:TPU:6 before, /device:TPU:1 now
where the time goes in v3:
time: 58.5 us; the launch traced here: 58 us
  starting transfers between devices  40.2 us (69%)
  waiting for transfers between devices  10 us (17%)
  Pallas kernels  5.38 us (9%)
  local copies, waits for them, and re-layouts  1.69 us (3%)
  between operations  0.74 us (1%)
    all_to_all x2, starting transfers between devices, exchange(): lax.all_to_all(x.reshape(NB, 1, NY), 'blk', split_axis=0, concat_axis=0,...  28.6 us
    all_to_all x2, waiting for transfers between devices, exchange(): lax.all_to_all(x.reshape(NB, 1, NY), 'blk', split_axis=0, concat_axis=0,...  7.71 us
    pallas_call x5, Pallas kernels, call(): pl.pallas_call(kernel, out_shape=[jax.ShapeDtypeStruct(s, d) for s, d in...  5.38 us
    ppermute x1, starting transfers between devices, body(): far = lax.ppermute(far, 'sub', swaps(4, 1))  3.72 us
    ppermute x1, starting transfers between devices, body(): near = lax.ppermute(near, 'sub', swaps(4, 0))  3.12 us
    ppermute x1, starting transfers between devices, body(): pair = lax.ppermute(pair, 'blk', swaps(NB, 0))  2.53 us
    ppermute x1, waiting for transfers between devices, body(): far = lax.ppermute(far, 'sub', swaps(4, 1))  2.29 us
    ppermute x1, starting transfers between devices, body(): cross = lax.ppermute(cross, 'blk', swaps(NB, 1))  2.2 us
  transfers between devices with their start and end apart: 6, of which 3 were waited for; matrix products, arithmetic and copies ran while one was open for 0% of the time, Pallas kernels for 0%

profile of v3, /device:TPU:1, one launch (start us, length us, event | category | flops | bytes accessed | tf_op | source)
XLA Modules:
  0.0 58.0 jit_solution(4982689766707887563)
XLA Ops:
  0.6 1.9 %pack.1 = (f32[128,128]{1,0:T(8,128)}, s32[1,512]{1,0:T(1,128)}, s32[1,512]{1,0:T(1,128)}) custom-call(s32[1,512]{1,0:T(1,128)} %bitcast.20, s32[1,512]{1,0:T(1,128)} %bitcast.21, f32[3,1,512]{2,1,0:T(1,128)} %bitcast.18, f32[3,1,512]{2,1,0:T(1,128)} %bitcast.19), custom_call_target="tpu_custom_call" | custom-call | flops 2000000 | bytes 2000000 | tf_op jit(solution)/shard_map/pack/pallas_call | solution.py:255
  2.5 0.0 copy-start.3
  2.5 18.8 %all-to-all-start = ((f32[128,1,128]{2,1,0:T(1,128)}), f32[128,1,128]{2,1,0:T(1,128)S(1)}, u32[]{:S(2)}, u32[]{:S(2)}) async-start(f32[128,1,128]{2,1,0:T(1,128)} %bitcast.17), calls=%async_computation | async-start | bytes 131072 | tf_op jit(solution)/shard_map/all_to_all | solution.py:269
  21.3 0.0 copy-start.2
  21.3 0.0 copy-done.3
  21.3 0.7 %copy-done.2 = s32[1,512]{1,0:T(1,128)S(1)} copy-done((s32[1,512]{1,0:T(1,128)S(1)}, s32[1,512]{1,0:T(1,128)}, u32[]{:S(2)}) %copy-start.2) | copy-done | bytes 2072
  22.0 0.0 copy-start
  22.0 1.0 %copy-done = f32[27,4,8,128]{3,2,1,0:T(8,128)S(1)} copy-done((f32[27,4,8,128]{3,2,1,0:T(8,128)S(1)}, f32[27,4,8,128]{3,2,1,0:T(8,128)}, u32[]{:S(2)}) %copy-start) | copy-done | bytes 442392
  23.0 0.0 copy-start.1
  23.0 0.1 velocity.1
  23.1 7.5 %all-to-all-done = f32[128,1,128]{2,1,0:T(1,128)S(1)} async-done(((f32[128,1,128]{2,1,0:T(1,128)}), f32[128,1,128]{2,1,0:T(1,128)S(1)}, u32[]{:S(2)}, u32[]{:S(2)}) %all-to-all-start) | async-done | bytes 65568 | tf_op jit(solution)/shard_map/all_to_all | solution.py:269
  30.7 0.0 copy-done.1
  30.7 1.9 %force.1 = (f32[27,4,8,128]{3,2,1,0:T(8,128)S(1)}, f32[128,128]{1,0:T(8,128)}, f32[9,8,128]{2,1,0:T(8,128)S(1)}, f32[9,8,128]{2,1,0:T(8,128)S(1)}) custom-call(f32[128,128]{1,0:T(8,128)S(1)} %bitcast.16, bf16[384,128]{1,0:T(8,128)(2,1)S(1)} %get-tuple-element.19.vel_ref, f32[27,4,8,128]{3,2,1,0:T(8,128)S(1)} %copy-done.1), custom_call_target="tpu_custom_call" | custom-call | flops 2000000 | bytes 2000000 | tf_op jit(solution)/shard_map/force/pallas_call | solution.py:255
  32.5 2.5 %collective-permute-start = (f32[9,8,128]{2,1,0:T(8,128)S(1)}, f32[9,8,128]{2,1,0:T(8,128)S(1)}, u32[]{:S(2)}, u32[]{:S(2)}) collective-permute-start(f32[9,8,128]{2,1,0:T(8,128)S(1)} %get-tuple-element.21), channel_id=1, source_target_pairs={{0,4},{8,12},{16,20},{24,28},{32,36},{40,44},{48,52},{56,60},{64,6... | collective-permute-start | bytes 110600 | tf_op jit(solution)/shard_map/ppermute | solution.py:296
  35.1 2.2 %collective-permute-start.1 = (f32[9,8,128]{2,1,0:T(8,128)S(1)}, f32[9,8,128]{2,1,0:T(8,128)S(1)}, u32[]{:S(2)}, u32[]{:S(2)}) collective-permute-start(f32[9,8,128]{2,1,0:T(8,128)S(1)} %get-tuple-element.22), channel_id=1, source_target_pairs={{4,8},{12,16},{20,24},{28,32},{36,40},{44,48},{52,56},{60,64},{68,... | collective-permute-start | bytes 110600 | tf_op jit(solution)/shard_map/ppermute | solution.py:295
  37.3 9.9 %all-to-all-start.1 = ((f32[128,1,128]{2,1,0:T(1,128)}), f32[128,1,128]{2,1,0:T(1,128)S(1)}, u32[]{:S(2)}, u32[]{:S(2)}) async-start(f32[128,1,128]{2,1,0:T(1,128)} %bitcast.8), calls=%async_computation.1 | async-start | bytes 131072 | tf_op jit(solution)/shard_map/all_to_all | solution.py:269
  47.2 0.0 collective-permute-done.low_ref
  47.2 0.0 collective-permute-done.1.high_ref
  47.2 3.1 %collective-permute-start.2 = (f32[36,128]{1,0:T(8,128)S(1)}, f32[36,128]{1,0:T(8,128)S(1)}, u32[]{:S(2)}, u32[]{:S(2)}) collective-permute-start(f32[36,128]{1,0:T(8,128)S(1)} %get-tuple-element.23), channel_id=1, source_target_pairs={{0,1},{2,3},{1,0},{3,2},{4,5},{6,7},{5,4},{7,6},{8,9},{10,11},{9,8... | collective-permute-start | bytes 55304 | tf_op jit(solution)/shard_map/ppermute | solution.py:299
  50.3 3.7 %collective-permute-start.3 = (f32[36,128]{1,0:T(8,128)S(1)}, f32[36,128]{1,0:T(8,128)S(1)}, u32[]{:S(2)}, u32[]{:S(2)}) collective-permute-start(f32[36,128]{1,0:T(8,128)S(1)} %get-tuple-element.24), channel_id=1, source_target_pairs={{1,2},{3,0},{2,1},{0,3},{5,6},{7,4},{6,5},{4,7},{9,10},{11,8},{10,... | collective-permute-start | bytes 55304 | tf_op jit(solution)/shard_map/ppermute | solution.py:300
  54.1 0.0 collective-permute-done.2.near_ref
  54.1 2.3 %collective-permute-done.3.far_ref = f32[36,128]{1,0:T(8,128)S(1)} collective-permute-done((f32[36,128]{1,0:T(8,128)S(1)}, f32[36,128]{1,0:T(8,128)S(1)}, u32[]{:S(2)}, u32[]{:S(2)}) %collective-permute-start.3) | collective-permute-done | bytes 18464 | tf_op jit(solution)/shard_map/ppermute | solution.py:300
  56.4 0.2 all-to-all-done.1
  56.5 1.5 %last.1 = (f32[27,4,8,128]{3,2,1,0:T(8,128)}, f32[3,1,512]{2,1,0:T(1,128)}) custom-call(f32[27,4,8,128]{3,2,1,0:T(8,128)S(1)} %get-tuple-element.20.post_ref, f32[9,8,128]{2,1,0:T(8,128)S(1)} %collective-permute-done.low_ref, f32[9,8,128]{2,1,0:T(8,128)S(1)} %collective-permute-done.1.high_ref, f32[36,128]{1,0:T(8,128)S(1)} %collective-permute-done.2.near_ref, ...), custom_call_target="tpu_custom_call" | custom-call | flops 2000000 | bytes 2000000 | tf_op jit(solution)/shard_map/last/pallas_call | solution.py:255
  (1 shorter events, 0.0 us)
Async XLA Ops:
  2.5 18.8 %copy-start.3 = (s32[1,512]{1,0:T(1,128)S(1)}, s32[1,512]{1,0:T(1,128)}, u32[]{:S(2)}) copy-start(s32[1,512]{1,0:T(1,128)} %get-tuple-element.18.rank_in) | copy-start | bytes 6148
  2.5 28.1 %all-to-all-start = ((f32[128,1,128]{2,1,0:T(1,128)}), f32[128,1,128]{2,1,0:T(1,128)S(1)}, u32[]{:S(2)}, u32[]{:S(2)}) async-start(f32[128,1,128]{2,1,0:T(1,128)} %bitcast.17), calls=%async_computation | async-start | bytes 131072 | tf_op jit(solution)/shard_map/all_to_all | solution.py:269
  21.3 0.7 %copy-start.2 = (s32[1,512]{1,0:T(1,128)S(1)}, s32[1,512]{1,0:T(1,128)}, u32[]{:S(2)}) copy-start(s32[1,512]{1,0:T(1,128)} %get-tuple-element.17.row_in) | copy-start | bytes 6148
  22.0 1.0 %copy-start = (f32[27,4,8,128]{3,2,1,0:T(8,128)S(1)}, f32[27,4,8,128]{3,2,1,0:T(8,128)}, u32[]{:S(2)}) copy-start(f32[27,4,8,128]{3,2,1,0:T(8,128)} %pop_ref.3) | copy-start | bytes 1327108
  23.0 7.7 %copy-start.1 = (f32[27,4,8,128]{3,2,1,0:T(8,128)S(1)}, f32[27,4,8,128]{3,2,1,0:T(8,128)}, u32[]{:S(2)}) copy-start(f32[27,4,8,128]{3,2,1,0:T(8,128)} %pop_ref.3) | copy-start | bytes 1327108
  32.5 14.6 %collective-permute-start = (f32[9,8,128]{2,1,0:T(8,128)S(1)}, f32[9,8,128]{2,1,0:T(8,128)S(1)}, u32[]{:S(2)}, u32[]{:S(2)}) collective-permute-start(f32[9,8,128]{2,1,0:T(8,128)S(1)} %get-tuple-element.21), channel_id=1, source_target_pairs={{0,4},{8,12},{16,20},{24,28},{32,36},{40,44},{48,52},{56,60},{64,6... | collective-permute-start | bytes 110600 | tf_op jit(solution)/shard_map/ppermute | solution.py:296
  35.1 12.1 %collective-permute-start.1 = (f32[9,8,128]{2,1,0:T(8,128)S(1)}, f32[9,8,128]{2,1,0:T(8,128)S(1)}, u32[]{:S(2)}, u32[]{:S(2)}) collective-permute-start(f32[9,8,128]{2,1,0:T(8,128)S(1)} %get-tuple-element.22), channel_id=1, source_target_pairs={{4,8},{12,16},{20,24},{28,32},{36,40},{44,48},{52,56},{60,64},{68,... | collective-permute-start | bytes 110600 | tf_op jit(solution)/shard_map/ppermute | solution.py:295
  37.3 19.2 %all-to-all-start.1 = ((f32[128,1,128]{2,1,0:T(1,128)}), f32[128,1,128]{2,1,0:T(1,128)S(1)}, u32[]{:S(2)}, u32[]{:S(2)}) async-start(f32[128,1,128]{2,1,0:T(1,128)} %bitcast.8), calls=%async_computation.1 | async-start | bytes 131072 | tf_op jit(solution)/shard_map/all_to_all | solution.py:269
  47.2 6.9 %collective-permute-start.2 = (f32[36,128]{1,0:T(8,128)S(1)}, f32[36,128]{1,0:T(8,128)S(1)}, u32[]{:S(2)}, u32[]{:S(2)}) collective-permute-start(f32[36,128]{1,0:T(8,128)S(1)} %get-tuple-element.23), channel_id=1, source_target_pairs={{0,1},{2,3},{1,0},{3,2},{4,5},{6,7},{5,4},{7,6},{8,9},{10,11},{9,8... | collective-permute-start | bytes 55304 | tf_op jit(solution)/shard_map/ppermute | solution.py:299
  50.3 6.0 %collective-permute-start.3 = (f32[36,128]{1,0:T(8,128)S(1)}, f32[36,128]{1,0:T(8,128)S(1)}, u32[]{:S(2)}, u32[]{:S(2)}) collective-permute-start(f32[36,128]{1,0:T(8,128)S(1)} %get-tuple-element.24), channel_id=1, source_target_pairs={{1,2},{3,0},{2,1},{0,3},{5,6},{7,4},{6,5},{4,7},{9,10},{11,8},{10,... | collective-permute-start | bytes 55304 | tf_op jit(solution)/shard_map/ppermute | solution.py:300

commit v4 on v3

--- a/solution.py
+++ b/solution.py
@@ -22,7 +22,8 @@
 DOWN_Z = [i for i in range(27) if VEL[i][2] == -1]
 LIMIT = 12 * 1024 * 1024
 FIRST = 56 * 1024 * 1024
-TURN = 112
+TURN = 127
+BACK = 113
 EDGE = 2_000_000_000
 
 
@@ -45,7 +46,7 @@
 
 def pack_kernel(dest_ref, cell_ref, offs_ref, targ_ref, send_ref, row_ref, rank_ref):
     owner = (dest_ref[...] - TURN) & (NB - 1)
-    row_ref[...] = owner
+    row_ref[...] = (dest_ref[...] - BACK) & (NB - 1)
     hot = jnp.where(iota((NB, M), 0) == owner, 1.0, 0.0)
     hot16 = hot.astype(BF16)
     blocks = [slice(NB * k, NB * k + NB) for k in range(M // NB)]
@@ -155,6 +156,8 @@
         near.append(jnp.concatenate(col0, axis=0))
         far.append(jnp.concatenate(col1, axis=0))
     reply = jnp.concatenate([p for comp in pulls for p in comp] + [jnp.zeros((NB - 24, NB), F32)], axis=0)
+    if TURN != BACK:
+        reply = pltpu.roll(reply, (TURN - BACK) % NB, 1)
     back_ref[...] = jnp.transpose(reply)
     sent = pltpu.make_async_copy(back_ref, back_hbm, sem)
     sent.start()
@@ -264,8 +267,8 @@
     )(*args)
 
 
-def exchange(x):
-    order = [(k + TURN) % NB for k in range(NB)]
+def exchange(x, turn):
+    order = [(k + turn) % NB for k in range(NB)]
     out = lax.all_to_all(x.reshape(NB, 1, NY), "blk", split_axis=0, concat_axis=0, tiled=True, axis_index_groups=[order])
     return out.reshape(NB, NY)
 
@@ -281,7 +284,7 @@
     offs = offsets.reshape(3, 1, M)
     targ = target.reshape(3, 1, M)
     send, row, rank = call(pack_kernel, [((NB, NY), F32), ((1, M), jnp.int32), ((1, M), jnp.int32)], dest, cell, offs, targ, name="pack", limit=FIRST)
-    recv = exchange(send)
+    recv = exchange(send, TURN)
     ints = ((1, M), jnp.int32)
     vel, row, rank = call(velocity_kernel, [((384, NY), BF16), ints, ints], populations, row, rank, name="velocity")
     face = (9, ZD, NY)
@@ -291,7 +294,7 @@
         recv, vel, populations, name="force", far=(1,),
         scratch=[pltpu.VMEM((NB, NY), F32), pltpu.SemaphoreType.DMA],
     )
-    reply = exchange(back)
+    reply = exchange(back, BACK)
     cross = lax.ppermute(cross, "blk", swaps(NB, 1))
     pair = lax.ppermute(pair, "blk", swaps(NB, 0))
     edge = (36, NY)

time: 58.5 us -> 55.9 us (0.956)
  waiting for transfers between devices: 10 us -> 7.86 us
    all_to_all x2, waiting for transfers between devices: 7.71 us -> 5.56 us  [exchange(): lax.all_to_all(x.reshape(NB, 1, NY), 'blk', split_axis=0, concat_axis=0,...]
where the time goes in v4:
time: 55.9 us; the launch traced here: 55.5 us
  starting transfers between devices  39.8 us (71%)
  waiting for transfers between devices  7.86 us (14%)
  Pallas kernels  5.37 us (10%)
  local copies, waits for them, and re-layouts  1.69 us (3%)
  between operations  0.74 us (1%)
    all_to_all x2, starting transfers between devices, exchange(): lax.all_to_all(x.reshape(NB, 1, NY), 'blk', split_axis=0, concat_axis=0,...  28.2 us
    all_to_all x2, waiting for transfers between devices, exchange(): lax.all_to_all(x.reshape(NB, 1, NY), 'blk', split_axis=0, concat_axis=0,...  5.56 us
    pallas_call x5, Pallas kernels, call(): pl.pallas_call(kernel, out_shape=[jax.ShapeDtypeStruct(s, d) for s, d in...  5.37 us
    ppermute x1, starting transfers between devices, body(): far = lax.ppermute(far, 'sub', swaps(4, 1))  3.72 us
    ppermute x1, starting transfers between devices, body(): near = lax.ppermute(near, 'sub', swaps(4, 0))  3.12 us
    ppermute x1, starting transfers between devices, body(): pair = lax.ppermute(pair, 'blk', swaps(NB, 0))  2.54 us
    ppermute x1, waiting for transfers between devices, body(): far = lax.ppermute(far, 'sub', swaps(4, 1))  2.29 us
    ppermute x1, starting transfers between devices, body(): cross = lax.ppermute(cross, 'blk', swaps(NB, 1))  2.23 us
  transfers between devices with their start and end apart: 6, of which 3 were waited for; matrix products, arithmetic and copies ran while one was open for 0% of the time, Pallas kernels for 0%

profile of v4, /device:TPU:1, one launch (start us, length us, event | category | flops | bytes accessed | tf_op | source)
XLA Modules:
  0.0 55.5 jit_solution(2109021090037328082)
XLA Ops:
  0.6 1.9 %pack.1 = (f32[128,128]{1,0:T(8,128)}, s32[1,512]{1,0:T(1,128)}, s32[1,512]{1,0:T(1,128)}) custom-call(s32[1,512]{1,0:T(1,128)} %bitcast.20, s32[1,512]{1,0:T(1,128)} %bitcast.21, f32[3,1,512]{2,1,0:T(1,128)} %bitcast.18, f32[3,1,512]{2,1,0:T(1,128)} %bitcast.19), custom_call_target="tpu_custom_call" | custom-call | flops 2000000 | bytes 2000000 | tf_op jit(solution)/shard_map/pack/pallas_call | solution.py:258
  2.5 0.0 copy-start.3
  2.5 18.5 %all-to-all-start = ((f32[128,1,128]{2,1,0:T(1,128)}), f32[128,1,128]{2,1,0:T(1,128)S(1)}, u32[]{:S(2)}, u32[]{:S(2)}) async-start(f32[128,1,128]{2,1,0:T(1,128)} %bitcast.17), calls=%async_computation | async-start | bytes 131072 | tf_op jit(solution)/shard_map/all_to_all | solution.py:272
  21.0 0.0 copy-start.2
  21.0 0.0 copy-done.3
  21.0 0.7 %copy-done.2 = s32[1,512]{1,0:T(1,128)S(1)} copy-done((s32[1,512]{1,0:T(1,128)S(1)}, s32[1,512]{1,0:T(1,128)}, u32[]{:S(2)}) %copy-start.2) | copy-done | bytes 2072
  21.7 0.0 copy-start
  21.7 1.0 %copy-done = f32[27,4,8,128]{3,2,1,0:T(8,128)S(1)} copy-done((f32[27,4,8,128]{3,2,1,0:T(8,128)S(1)}, f32[27,4,8,128]{3,2,1,0:T(8,128)}, u32[]{:S(2)}) %copy-start) | copy-done | bytes 442392
  22.7 0.0 copy-start.1
  22.7 0.1 velocity.1
  22.8 5.4 %all-to-all-done = f32[128,1,128]{2,1,0:T(1,128)S(1)} async-done(((f32[128,1,128]{2,1,0:T(1,128)}), f32[128,1,128]{2,1,0:T(1,128)S(1)}, u32[]{:S(2)}, u32[]{:S(2)}) %all-to-all-start) | async-done | bytes 65568 | tf_op jit(solution)/shard_map/all_to_all | solution.py:272
  28.2 0.0 copy-done.1
  28.2 1.9 %force.1 = (f32[27,4,8,128]{3,2,1,0:T(8,128)S(1)}, f32[128,128]{1,0:T(8,128)}, f32[9,8,128]{2,1,0:T(8,128)S(1)}, f32[9,8,128]{2,1,0:T(8,128)S(1)}) custom-call(f32[128,128]{1,0:T(8,128)S(1)} %bitcast.16, bf16[384,128]{1,0:T(8,128)(2,1)S(1)} %get-tuple-element.19.vel_ref, f32[27,4,8,128]{3,2,1,0:T(8,128)S(1)} %copy-done.1), custom_call_target="tpu_custom_call" | custom-call | flops 2000000 | bytes 2000000 | tf_op jit(solution)/shard_map/force/pallas_call | solution.py:258
  30.1 2.5 %collective-permute-start = (f32[9,8,128]{2,1,0:T(8,128)S(1)}, f32[9,8,128]{2,1,0:T(8,128)S(1)}, u32[]{:S(2)}, u32[]{:S(2)}) collective-permute-start(f32[9,8,128]{2,1,0:T(8,128)S(1)} %get-tuple-element.21), channel_id=1, source_target_pairs={{0,4},{8,12},{16,20},{24,28},{32,36},{40,44},{48,52},{56,60},{64,6... | collective-permute-start | bytes 110600 | tf_op jit(solution)/shard_map/ppermute | solution.py:299
  32.7 2.2 %collective-permute-start.1 = (f32[9,8,128]{2,1,0:T(8,128)S(1)}, f32[9,8,128]{2,1,0:T(8,128)S(1)}, u32[]{:S(2)}, u32[]{:S(2)}) collective-permute-start(f32[9,8,128]{2,1,0:T(8,128)S(1)} %get-tuple-element.22), channel_id=1, source_target_pairs={{4,8},{12,16},{20,24},{28,32},{36,40},{44,48},{52,56},{60,64},{68,... | collective-permute-start | bytes 110600 | tf_op jit(solution)/shard_map/ppermute | solution.py:298
  34.9 9.7 %all-to-all-start.1 = ((f32[128,1,128]{2,1,0:T(1,128)}), f32[128,1,128]{2,1,0:T(1,128)S(1)}, u32[]{:S(2)}, u32[]{:S(2)}) async-start(f32[128,1,128]{2,1,0:T(1,128)} %bitcast.8), calls=%async_computation.1 | async-start | bytes 131072 | tf_op jit(solution)/shard_map/all_to_all | solution.py:272
  44.6 0.0 collective-permute-done.low_ref
  44.6 0.0 collective-permute-done.1.high_ref
  44.7 3.1 %collective-permute-start.2 = (f32[36,128]{1,0:T(8,128)S(1)}, f32[36,128]{1,0:T(8,128)S(1)}, u32[]{:S(2)}, u32[]{:S(2)}) collective-permute-start(f32[36,128]{1,0:T(8,128)S(1)} %get-tuple-element.23), channel_id=1, source_target_pairs={{0,1},{2,3},{1,0},{3,2},{4,5},{6,7},{5,4},{7,6},{8,9},{10,11},{9,8... | collective-permute-start | bytes 55304 | tf_op jit(solution)/shard_map/ppermute | solution.py:302
  47.8 3.7 %collective-permute-start.3 = (f32[36,128]{1,0:T(8,128)S(1)}, f32[36,128]{1,0:T(8,128)S(1)}, u32[]{:S(2)}, u32[]{:S(2)}) collective-permute-start(f32[36,128]{1,0:T(8,128)S(1)} %get-tuple-element.24), channel_id=1, source_target_pairs={{1,2},{3,0},{2,1},{0,3},{5,6},{7,4},{6,5},{4,7},{9,10},{11,8},{10,... | collective-permute-start | bytes 55304 | tf_op jit(solution)/shard_map/ppermute | solution.py:303
  51.5 0.0 collective-permute-done.2.near_ref
  51.5 2.3 %collective-permute-done.3.far_ref = f32[36,128]{1,0:T(8,128)S(1)} collective-permute-done((f32[36,128]{1,0:T(8,128)S(1)}, f32[36,128]{1,0:T(8,128)S(1)}, u32[]{:S(2)}, u32[]{:S(2)}) %collective-permute-start.3) | collective-permute-done | bytes 18464 | tf_op jit(solution)/shard_map/ppermute | solution.py:303
  53.8 0.2 all-to-all-done.1
  54.0 1.5 %last.1 = (f32[27,4,8,128]{3,2,1,0:T(8,128)}, f32[3,1,512]{2,1,0:T(1,128)}) custom-call(f32[27,4,8,128]{3,2,1,0:T(8,128)S(1)} %get-tuple-element.20.post_ref, f32[9,8,128]{2,1,0:T(8,128)S(1)} %collective-permute-done.low_ref, f32[9,8,128]{2,1,0:T(8,128)S(1)} %collective-permute-done.1.high_ref, f32[36,128]{1,0:T(8,128)S(1)} %collective-permute-done.2.near_ref, ...), custom_call_target="tpu_custom_call" | custom-call | flops 2000000 | bytes 2000000 | tf_op jit(solution)/shard_map/last/pallas_call | solution.py:258
  (1 shorter events, 0.0 us)
Async XLA Ops:
  2.5 18.5 %copy-start.3 = (s32[1,512]{1,0:T(1,128)S(1)}, s32[1,512]{1,0:T(1,128)}, u32[]{:S(2)}) copy-start(s32[1,512]{1,0:T(1,128)} %get-tuple-element.18.rank_in) | copy-start | bytes 6148
  2.5 25.7 %all-to-all-start = ((f32[128,1,128]{2,1,0:T(1,128)}), f32[128,1,128]{2,1,0:T(1,128)S(1)}, u32[]{:S(2)}, u32[]{:S(2)}) async-start(f32[128,1,128]{2,1,0:T(1,128)} %bitcast.17), calls=%async_computation | async-start | bytes 131072 | tf_op jit(solution)/shard_map/all_to_all | solution.py:272
  21.0 0.7 %copy-start.2 = (s32[1,512]{1,0:T(1,128)S(1)}, s32[1,512]{1,0:T(1,128)}, u32[]{:S(2)}) copy-start(s32[1,512]{1,0:T(1,128)} %get-tuple-element.17.row_in) | copy-start | bytes 6148
  21.7 1.0 %copy-start = (f32[27,4,8,128]{3,2,1,0:T(8,128)S(1)}, f32[27,4,8,128]{3,2,1,0:T(8,128)}, u32[]{:S(2)}) copy-start(f32[27,4,8,128]{3,2,1,0:T(8,128)} %pop_ref.3) | copy-start | bytes 1327108
  22.7 5.5 %copy-start.1 = (f32[27,4,8,128]{3,2,1,0:T(8,128)S(1)}, f32[27,4,8,128]{3,2,1,0:T(8,128)}, u32[]{:S(2)}) copy-start(f32[27,4,8,128]{3,2,1,0:T(8,128)} %pop_ref.3) | copy-start | bytes 1327108
  30.1 14.5 %collective-permute-start = (f32[9,8,128]{2,1,0:T(8,128)S(1)}, f32[9,8,128]{2,1,0:T(8,128)S(1)}, u32[]{:S(2)}, u32[]{:S(2)}) collective-permute-start(f32[9,8,128]{2,1,0:T(8,128)S(1)} %get-tuple-element.21), channel_id=1, source_target_pairs={{0,4},{8,12},{16,20},{24,28},{32,36},{40,44},{48,52},{56,60},{64,6... | collective-permute-start | bytes 110600 | tf_op jit(solution)/shard_map/ppermute | solution.py:299
  32.7 12.0 %collective-permute-start.1 = (f32[9,8,128]{2,1,0:T(8,128)S(1)}, f32[9,8,128]{2,1,0:T(8,128)S(1)}, u32[]{:S(2)}, u32[]{:S(2)}) collective-permute-start(f32[9,8,128]{2,1,0:T(8,128)S(1)} %get-tuple-element.22), channel_id=1, source_target_pairs={{4,8},{12,16},{20,24},{28,32},{36,40},{44,48},{52,56},{60,64},{68,... | collective-permute-start | bytes 110600 | tf_op jit(solution)/shard_map/ppermute | solution.py:298
  34.9 19.1 %all-to-all-start.1 = ((f32[128,1,128]{2,1,0:T(1,128)}), f32[128,1,128]{2,1,0:T(1,128)S(1)}, u32[]{:S(2)}, u32[]{:S(2)}) async-start(f32[128,1,128]{2,1,0:T(1,128)} %bitcast.8), calls=%async_computation.1 | async-start | bytes 131072 | tf_op jit(solution)/shard_map/all_to_all | solution.py:272
  44.7 6.9 %collective-permute-start.2 = (f32[36,128]{1,0:T(8,128)S(1)}, f32[36,128]{1,0:T(8,128)S(1)}, u32[]{:S(2)}, u32[]{:S(2)}) collective-permute-start(f32[36,128]{1,0:T(8,128)S(1)} %get-tuple-element.23), channel_id=1, source_target_pairs={{0,1},{2,3},{1,0},{3,2},{4,5},{6,7},{5,4},{7,6},{8,9},{10,11},{9,8... | collective-permute-start | bytes 55304 | tf_op jit(solution)/shard_map/ppermute | solution.py:302
  47.8 6.0 %collective-permute-start.3 = (f32[36,128]{1,0:T(8,128)S(1)}, f32[36,128]{1,0:T(8,128)S(1)}, u32[]{:S(2)}, u32[]{:S(2)}) collective-permute-start(f32[36,128]{1,0:T(8,128)S(1)} %get-tuple-element.24), channel_id=1, source_target_pairs={{1,2},{3,0},{2,1},{0,3},{5,6},{7,4},{6,5},{4,7},{9,10},{11,8},{10,... | collective-permute-start | bytes 55304 | tf_op jit(solution)/shard_map/ppermute | solution.py:303

commit v5 on v4

--- a/solution.py
+++ b/solution.py
@@ -87,12 +87,14 @@
     return rho, jx, jy, jz
 
 
-def velocity_kernel(pop_ref, row_in, rank_in, vel_ref, row_ref, rank_ref):
+def velocity_kernel(pop_ref, row_in, rank_in, vel_ref, row_ref, rank_ref, mom_ref):
     row_ref[...] = row_in[...]
     rank_ref[...] = rank_in[...]
     comps = [[], [], []]
     for x in range(XD):
         rho, jx, jy, jz = moments(lambda i: pop_ref[i, x])
+        for k, v in enumerate((rho, jx, jy, jz, 1.0 / rho)):
+            mom_ref[k, x] = v
         for c, j in enumerate((jx, jy, jz)):
             comps[c].append(j / rho)
     low = jnp.concatenate([v for comp in comps for v in comp], axis=0)
@@ -110,7 +112,7 @@
     return total
 
 
-def force_kernel(recv_ref, vel_ref, pop_ref, post_ref, back_hbm, pair_ref, cross_ref, back_ref, sem):
+def force_kernel(recv_ref, vel_ref, pop_ref, mom_ref, post_ref, back_hbm, pair_ref, cross_ref, back_ref, sem):
     first = (lax.axis_index("blk") & 1) == 0
     table = jnp.transpose(recv_ref[...])
     feat = [table[8 * k : 8 * k + 8] for k in range(8)]
@@ -166,9 +168,8 @@
     field = dot_nt(hi, hot) + dot_nt(lo, hot)
     field = field[:96] + pltpu.roll(field[96:], 1, 1)
     for x in range(XD):
-        rho, jx, jy, jz = moments(lambda i: pop_ref[i, x])
+        rho, jx, jy, jz, inv = [mom_ref[k, x] for k in range(5)]
         force = [field[32 * c + 8 * x : 32 * c + 8 * x + 8] for c in range(3)]
-        inv = 1.0 / rho
         u = [(j + 0.5 * f) * inv for j, f in zip((jx, jy, jz), force)]
         usq = u[0] * u[0] + u[1] * u[1] + u[2] * u[2]
         uf = u[0] * force[0] + u[1] * force[1] + u[2] * force[2]
@@ -286,12 +287,12 @@
     send, row, rank = call(pack_kernel, [((NB, NY), F32), ((1, M), jnp.int32), ((1, M), jnp.int32)], dest, cell, offs, targ, name="pack", limit=FIRST)
     recv = exchange(send, TURN)
     ints = ((1, M), jnp.int32)
-    vel, row, rank = call(velocity_kernel, [((384, NY), BF16), ints, ints], populations, row, rank, name="velocity")
+    vel, row, rank, mom = call(velocity_kernel, [((384, NY), BF16), ints, ints, ((5, XD, ZD, NY), F32)], populations, row, rank, name="velocity")
     face = (9, ZD, NY)
     post, back, pair, cross = call(
         force_kernel,
         [((27, XD, ZD, NY), F32), ((NB, NY), F32), (face, F32), (face, F32)],
-        recv, vel, populations, name="force", far=(1,),
+        recv, vel, populations, mom, name="force", far=(1,),
         scratch=[pltpu.VMEM((NB, NY), F32), pltpu.SemaphoreType.DMA],
     )
     reply = exchange(back, BACK)

time: 55.9 us -> 55.9 us (level)
  no operation moved by 1% of the time
where the time goes in v5:
time: 55.9 us; the launch traced here: 55.5 us
  starting transfers between devices  39.8 us (71%)
  waiting for transfers between devices  7.86 us (14%)
  Pallas kernels  5.37 us (10%)
  local copies, waits for them, and re-layouts  1.69 us (3%)
  between operations  0.75 us (1%)
    all_to_all x2, starting transfers between devices, exchange(): lax.all_to_all(x.reshape(NB, 1, NY), 'blk', split_axis=0, concat_axis=0,...  28.2 us
    all_to_all x2, waiting for transfers between devices, exchange(): lax.all_to_all(x.reshape(NB, 1, NY), 'blk', split_axis=0, concat_axis=0,...  5.56 us
    pallas_call x5, Pallas kernels, call(): pl.pallas_call(kernel, out_shape=[jax.ShapeDtypeStruct(s, d) for s, d in...  5.37 us
    ppermute x1, starting transfers between devices, body(): far = lax.ppermute(far, 'sub', swaps(4, 1))  3.72 us
    ppermute x1, starting transfers between devices, body(): near = lax.ppermute(near, 'sub', swaps(4, 0))  3.12 us
    ppermute x1, starting transfers between devices, body(): pair = lax.ppermute(pair, 'blk', swaps(NB, 0))  2.54 us
    ppermute x1, waiting for transfers between devices, body(): far = lax.ppermute(far, 'sub', swaps(4, 1))  2.29 us
    ppermute x1, starting transfers between devices, body(): cross = lax.ppermute(cross, 'blk', swaps(NB, 1))  2.23 us
  transfers between devices with their start and end apart: 6, of which 3 were waited for; matrix products, arithmetic and copies ran while one was open for 0% of the time, Pallas kernels for 0%

profile of v5, /device:TPU:1, one launch (start us, length us, event | category | flops | bytes accessed | tf_op | source)
XLA Modules:
  0.0 55.5 jit_solution(17087548733640000613)
XLA Ops:
  0.6 1.9 %pack.1 = (f32[128,128]{1,0:T(8,128)}, s32[1,512]{1,0:T(1,128)}, s32[1,512]{1,0:T(1,128)}) custom-call(s32[1,512]{1,0:T(1,128)} %bitcast.20, s32[1,512]{1,0:T(1,128)} %bitcast.21, f32[3,1,512]{2,1,0:T(1,128)} %bitcast.18, f32[3,1,512]{2,1,0:T(1,128)} %bitcast.19), custom_call_target="tpu_custom_call" | custom-call | flops 2000000 | bytes 2000000 | tf_op jit(solution)/shard_map/pack/pallas_call | solution.py:259
  2.5 0.0 copy-start.3
  2.5 18.5 %all-to-all-start = ((f32[128,1,128]{2,1,0:T(1,128)}), f32[128,1,128]{2,1,0:T(1,128)S(1)}, u32[]{:S(2)}, u32[]{:S(2)}) async-start(f32[128,1,128]{2,1,0:T(1,128)} %bitcast.17), calls=%async_computation | async-start | bytes 131072 | tf_op jit(solution)/shard_map/all_to_all | solution.py:273
  21.0 0.0 copy-start.2
  21.0 0.0 copy-done.3
  21.0 0.7 %copy-done.2 = s32[1,512]{1,0:T(1,128)S(1)} copy-done((s32[1,512]{1,0:T(1,128)S(1)}, s32[1,512]{1,0:T(1,128)}, u32[]{:S(2)}) %copy-start.2) | copy-done | bytes 2072
  21.7 0.0 copy-start
  21.7 1.0 %copy-done = f32[27,4,8,128]{3,2,1,0:T(8,128)S(1)} copy-done((f32[27,4,8,128]{3,2,1,0:T(8,128)S(1)}, f32[27,4,8,128]{3,2,1,0:T(8,128)}, u32[]{:S(2)}) %copy-start) | copy-done | bytes 442392
  22.7 0.0 copy-start.1
  22.7 0.1 velocity.1
  22.8 5.4 %all-to-all-done = f32[128,1,128]{2,1,0:T(1,128)S(1)} async-done(((f32[128,1,128]{2,1,0:T(1,128)}), f32[128,1,128]{2,1,0:T(1,128)S(1)}, u32[]{:S(2)}, u32[]{:S(2)}) %all-to-all-start) | async-done | bytes 65568 | tf_op jit(solution)/shard_map/all_to_all | solution.py:273
  28.2 0.0 copy-done.1
  28.2 1.9 %force.1 = (f32[27,4,8,128]{3,2,1,0:T(8,128)S(1)}, f32[128,128]{1,0:T(8,128)}, f32[9,8,128]{2,1,0:T(8,128)S(1)}, f32[9,8,128]{2,1,0:T(8,128)S(1)}) custom-call(f32[128,128]{1,0:T(8,128)S(1)} %bitcast.16, bf16[384,128]{1,0:T(8,128)(2,1)S(1)} %get-tuple-element.20.vel_ref, f32[27,4,8,128]{3,2,1,0:T(8,128)S(1)} %copy-done.1, ...), custom_call_target="tpu_custom_call" | custom-call | flops 2000000 | bytes 2000000 | tf_op jit(solution)/shard_map/force/pallas_call | solution.py:259
  30.1 2.5 %collective-permute-start = (f32[9,8,128]{2,1,0:T(8,128)S(1)}, f32[9,8,128]{2,1,0:T(8,128)S(1)}, u32[]{:S(2)}, u32[]{:S(2)}) collective-permute-start(f32[9,8,128]{2,1,0:T(8,128)S(1)} %get-tuple-element.23), channel_id=1, source_target_pairs={{0,4},{8,12},{16,20},{24,28},{32,36},{40,44},{48,52},{56,60},{64,6... | collective-permute-start | bytes 110600 | tf_op jit(solution)/shard_map/ppermute | solution.py:300
  32.7 2.2 %collective-permute-start.1 = (f32[9,8,128]{2,1,0:T(8,128)S(1)}, f32[9,8,128]{2,1,0:T(8,128)S(1)}, u32[]{:S(2)}, u32[]{:S(2)}) collective-permute-start(f32[9,8,128]{2,1,0:T(8,128)S(1)} %get-tuple-element.24), channel_id=1, source_target_pairs={{4,8},{12,16},{20,24},{28,32},{36,40},{44,48},{52,56},{60,64},{68,... | collective-permute-start | bytes 110600 | tf_op jit(solution)/shard_map/ppermute | solution.py:299
  34.9 9.7 %all-to-all-start.1 = ((f32[128,1,128]{2,1,0:T(1,128)}), f32[128,1,128]{2,1,0:T(1,128)S(1)}, u32[]{:S(2)}, u32[]{:S(2)}) async-start(f32[128,1,128]{2,1,0:T(1,128)} %bitcast.8), calls=%async_computation.1 | async-start | bytes 131072 | tf_op jit(solution)/shard_map/all_to_all | solution.py:273
  44.6 0.0 collective-permute-done.low_ref
  44.6 0.0 collective-permute-done.1.high_ref
  44.7 3.1 %collective-permute-start.2 = (f32[36,128]{1,0:T(8,128)S(1)}, f32[36,128]{1,0:T(8,128)S(1)}, u32[]{:S(2)}, u32[]{:S(2)}) collective-permute-start(f32[36,128]{1,0:T(8,128)S(1)} %get-tuple-element.25), channel_id=1, source_target_pairs={{0,1},{2,3},{1,0},{3,2},{4,5},{6,7},{5,4},{7,6},{8,9},{10,11},{9,8... | collective-permute-start | bytes 55304 | tf_op jit(solution)/shard_map/ppermute | solution.py:303
  47.8 3.7 %collective-permute-start.3 = (f32[36,128]{1,0:T(8,128)S(1)}, f32[36,128]{1,0:T(8,128)S(1)}, u32[]{:S(2)}, u32[]{:S(2)}) collective-permute-start(f32[36,128]{1,0:T(8,128)S(1)} %get-tuple-element.26), channel_id=1, source_target_pairs={{1,2},{3,0},{2,1},{0,3},{5,6},{7,4},{6,5},{4,7},{9,10},{11,8},{10,... | collective-permute-start | bytes 55304 | tf_op jit(solution)/shard_map/ppermute | solution.py:304
  51.5 0.0 collective-permute-done.2.near_ref
  51.5 2.3 %collective-permute-done.3.far_ref = f32[36,128]{1,0:T(8,128)S(1)} collective-permute-done((f32[36,128]{1,0:T(8,128)S(1)}, f32[36,128]{1,0:T(8,128)S(1)}, u32[]{:S(2)}, u32[]{:S(2)}) %collective-permute-start.3) | collective-permute-done | bytes 18464 | tf_op jit(solution)/shard_map/ppermute | solution.py:304
  53.8 0.2 all-to-all-done.1
  54.0 1.5 %last.1 = (f32[27,4,8,128]{3,2,1,0:T(8,128)}, f32[3,1,512]{2,1,0:T(1,128)}) custom-call(f32[27,4,8,128]{3,2,1,0:T(8,128)S(1)} %get-tuple-element.22.post_ref, f32[9,8,128]{2,1,0:T(8,128)S(1)} %collective-permute-done.low_ref, f32[9,8,128]{2,1,0:T(8,128)S(1)} %collective-permute-done.1.high_ref, f32[36,128]{1,0:T(8,128)S(1)} %collective-permute-done.2.near_ref, ...), custom_call_target="tpu_custom_call" | custom-call | flops 2000000 | bytes 2000000 | tf_op jit(solution)/shard_map/last/pallas_call | solution.py:259
  (1 shorter events, 0.0 us)
Async XLA Ops:
  2.5 18.5 %copy-start.3 = (s32[1,512]{1,0:T(1,128)S(1)}, s32[1,512]{1,0:T(1,128)}, u32[]{:S(2)}) copy-start(s32[1,512]{1,0:T(1,128)} %get-tuple-element.19.rank_in) | copy-start | bytes 6148
  2.5 25.7 %all-to-all-start = ((f32[128,1,128]{2,1,0:T(1,128)}), f32[128,1,128]{2,1,0:T(1,128)S(1)}, u32[]{:S(2)}, u32[]{:S(2)}) async-start(f32[128,1,128]{2,1,0:T(1,128)} %bitcast.17), calls=%async_computation | async-start | bytes 131072 | tf_op jit(solution)/shard_map/all_to_all | solution.py:273
  21.0 0.7 %copy-start.2 = (s32[1,512]{1,0:T(1,128)S(1)}, s32[1,512]{1,0:T(1,128)}, u32[]{:S(2)}) copy-start(s32[1,512]{1,0:T(1,128)} %get-tuple-element.18.row_in) | copy-start | bytes 6148
  21.7 1.0 %copy-start = (f32[27,4,8,128]{3,2,1,0:T(8,128)S(1)}, f32[27,4,8,128]{3,2,1,0:T(8,128)}, u32[]{:S(2)}) copy-start(f32[27,4,8,128]{3,2,1,0:T(8,128)} %pop_ref.3) | copy-start | bytes 1327108
  22.7 5.5 %copy-start.1 = (f32[27,4,8,128]{3,2,1,0:T(8,128)S(1)}, f32[27,4,8,128]{3,2,1,0:T(8,128)}, u32[]{:S(2)}) copy-start(f32[27,4,8,128]{3,2,1,0:T(8,128)} %pop_ref.3) | copy-start | bytes 1327108
  30.1 14.5 %collective-permute-start = (f32[9,8,128]{2,1,0:T(8,128)S(1)}, f32[9,8,128]{2,1,0:T(8,128)S(1)}, u32[]{:S(2)}, u32[]{:S(2)}) collective-permute-start(f32[9,8,128]{2,1,0:T(8,128)S(1)} %get-tuple-element.23), channel_id=1, source_target_pairs={{0,4},{8,12},{16,20},{24,28},{32,36},{40,44},{48,52},{56,60},{64,6... | collective-permute-start | bytes 110600 | tf_op jit(solution)/shard_map/ppermute | solution.py:300
  32.7 12.0 %collective-permute-start.1 = (f32[9,8,128]{2,1,0:T(8,128)S(1)}, f32[9,8,128]{2,1,0:T(8,128)S(1)}, u32[]{:S(2)}, u32[]{:S(2)}) collective-permute-start(f32[9,8,128]{2,1,0:T(8,128)S(1)} %get-tuple-element.24), channel_id=1, source_target_pairs={{4,8},{12,16},{20,24},{28,32},{36,40},{44,48},{52,56},{60,64},{68,... | collective-permute-start | bytes 110600 | tf_op jit(solution)/shard_map/ppermute | solution.py:299
  34.9 19.1 %all-to-all-start.1 = ((f32[128,1,128]{2,1,0:T(1,128)}), f32[128,1,128]{2,1,0:T(1,128)S(1)}, u32[]{:S(2)}, u32[]{:S(2)}) async-start(f32[128,1,128]{2,1,0:T(1,128)} %bitcast.8), calls=%async_computation.1 | async-start | bytes 131072 | tf_op jit(solution)/shard_map/all_to_all | solution.py:273
  44.7 6.9 %collective-permute-start.2 = (f32[36,128]{1,0:T(8,128)S(1)}, f32[36,128]{1,0:T(8,128)S(1)}, u32[]{:S(2)}, u32[]{:S(2)}) collective-permute-start(f32[36,128]{1,0:T(8,128)S(1)} %get-tuple-element.25), channel_id=1, source_target_pairs={{0,1},{2,3},{1,0},{3,2},{4,5},{6,7},{5,4},{7,6},{8,9},{10,11},{9,8... | collective-permute-start | bytes 55304 | tf_op jit(solution)/shard_map/ppermute | solution.py:303
  47.8 6.0 %collective-permute-start.3 = (f32[36,128]{1,0:T(8,128)S(1)}, f32[36,128]{1,0:T(8,128)S(1)}, u32[]{:S(2)}, u32[]{:S(2)}) collective-permute-start(f32[36,128]{1,0:T(8,128)S(1)} %get-tuple-element.26), channel_id=1, source_target_pairs={{1,2},{3,0},{2,1},{0,3},{5,6},{7,4},{6,5},{4,7},{9,10},{11,8},{10,... | collective-permute-start | bytes 55304 | tf_op jit(solution)/shard_map/ppermute | solution.py:304
